TPU v7x, 32 devices: a whole 2x2x4 slice. The times are simulated.
32 devices in a mesh: pair: 16 (over z, y, x), int: 2 (over core).
Axes of the slice: x: 2, y: 2, z: 4, core: 2. Of those that a mesh axis runs over, the one named last changes fastest.
Arguments:
- amps: bfloat16 [128, 64, 4096], P('pair', None, 'int'), may hold values from -6 to 6
- amp_mask: int32 [128, 64], P('pair'), may hold values 0 or 1
- integrals: bfloat16 [64, 4096, 4096], P('pair', None, 'int'), may hold values from -0.09375 to 0.09375
- block_mask: int32 [64], P('pair'), may hold values 0 or 1
- in_tiles: int32 [64], replicated, may hold values from 0 to 63, each once
- out_tiles: int32 [64], replicated, may hold values from 0 to 63, each once
- vir_energy: float32 [1024], replicated, may hold values from 0.5 to 3
- pair_energy: float32 [128], P('pair'), may hold values from -4 to -1
- dressing: bfloat16 [1024, 1024], P('pair'), may hold values from -0.1875 to 0.1875
Outputs:
- new_amps: bfloat16 [128, 64, 4096], P('pair', None, 'int')
Inputs may be any that keep to these rules, and one draw needn't show every extreme that they name: `in_tiles`: a permutation of the 64 tiles. `out_tiles`: a permutation of the 64 tiles.
All inputs are finite; a program needn't handle non-finite values. No bound on the sum of `amp_mask` or of `block_mask` on one device may be relied on, other than what follows from the above.
Results may differ from a plain program's by a relative error of at most 0.0038.
Values may be sent and summed in bfloat16 or wider, within the bound.
No kernel may reach another device: no remote copies, remote signals or barrier semaphores. Data moves between devices by JAX's collectives and lax.ppermute only.
A program may use at most 192 MiB of HBM per device.

v0:
```python
import jax
import jax.numpy as jnp
from jax import lax
from jax.sharding import PartitionSpec as P

TILE = 64
VT = 16
WA = 4


def shards(
    amps, amp_mask, integrals, block_mask, in_tiles, out_tiles, vir_energy, pair_energy, dressing
):
    local_pairs, tile_count, share_size = amps.shape
    strip_rows = share_size // TILE
    int_index = lax.axis_index("int")
    masked = jnp.where(amp_mask[:, :, None] > 0, amps, jnp.zeros_like(amps))
    ordered = jnp.take(masked, in_tiles, axis=1)
    received = lax.all_to_all(ordered, "pair", split_axis=1, concat_axis=0, tiled=True)
    partial_value = jnp.einsum(
        "psk,sak->psa", received, integrals, preferred_element_type=jnp.float32
    )
    partial_value = partial_value * block_mask.astype(jnp.float32)[None, :, None]
    partial_value = lax.optimization_barrier(partial_value.astype(jnp.bfloat16)).astype(jnp.float32)
    summed = lax.psum(partial_value.astype(jnp.bfloat16), "int").astype(jnp.float32)
    own_share = lax.dynamic_slice_in_dim(summed, int_index * share_size, share_size, 2)
    returned = lax.all_to_all(
        own_share.astype(jnp.bfloat16), "pair", split_axis=0, concat_axis=1, tiled=True
    ).astype(own_share.dtype)
    slot_of = (
        jnp.zeros((tile_count,), jnp.int32)
        .at[out_tiles]
        .set(jnp.arange(tile_count, dtype=jnp.int32))
    )
    ladder_terms = jnp.take(returned, slot_of, axis=1)
    tile_rows = masked.reshape(local_pairs, WA, VT, strip_rows, TILE)
    tile_rows = jnp.transpose(tile_rows, (0, 1, 3, 2, 4)).reshape(
        local_pairs * WA * strip_rows, VT * TILE
    )
    running = jnp.dot(
        tile_rows,
        lax.all_gather(dressing, "pair", axis=0, tiled=True),
        preferred_element_type=jnp.float32,
    )
    running = running.reshape(local_pairs, WA, strip_rows, VT, TILE)
    cycle_terms = jnp.transpose(running, (0, 1, 3, 2, 4)).reshape(
        local_pairs, tile_count, share_size
    )
    energies = vir_energy.reshape(VT, TILE)
    own_energy = lax.dynamic_slice_in_dim(energies[:WA], int_index * strip_rows, strip_rows, 1)
    denominator = (
        pair_energy[:, None, None, None, None]
        - own_energy[None, :, None, :, None]
        - energies[None, None, :, None, :]
    )
    denominator = denominator.reshape(local_pairs, tile_count, share_size)
    updated = masked.astype(jnp.float32) + (ladder_terms + cycle_terms) / denominator
    return updated.astype(jnp.bfloat16)


def solution(mesh):
    in_specs = (
        P("pair", None, "int"),
        P("pair", None),
        P("pair", None, "int"),
        P("pair"),
        P(),
        P(),
        P(),
        P("pair"),
        P("pair", None),
    )
    out_specs = P("pair", None, "int")
    return jax.shard_map(shards, mesh=mesh, in_specs=in_specs, out_specs=out_specs, check_vma=False)
```

profile of v0, /device:TPU:0, one launch (start us, length us, event | category | flops | bytes accessed | tf_op | source)
XLA Modules:
  0.0 238.4 jit_solution(3979288198121408598)
XLA Ops:
  7.4 0.7 broadcast_compare_fusion
  8.1 0.1 copy.29
  8.2 0.7 compare_and_fusion
  8.8 0.7 compare_select_fusion
  9.5 2.8 %copy_select_fusion = bf16[8,64,2048]{2,0,1:T(8,128)(2,1)S(1)} fusion(bf16[8,64,2048]{2,1,0:T(8,128)(2,1)} %param.9, pred[8,64]{0,1:T(8,128)(4,1)S(1)} %copy.29), kind=kLoop, calls=%fused_computation.15 | loop fusion | flops 1048576 | bytes 4194816 | tf_op jit(solution)/shard_map/jit(_where)/select_n | solution.py:17
  12.4 0.0 copy-start
  12.4 2.0 gather_fusion
  14.4 0.0 copy-done
  14.4 3.2 %select_bitcast_fusion = bf16[8,64,2048]{2,0,1:T(8,128)(2,1)} fusion(bf16[64,8,2048]{2,1,0:T(8,128)(2,1)} %gather_fusion, pred[64]{0:T(512)(128)(4,1)S(1)} %compare_and_fusion), kind=kLoop, calls=%fused_computation.16 | loop fusion | flops 1048576 | bytes 4194368 | tf_op jit(solution)/shard_map/jit(_take)/select_n | solution.py:18
  17.6 0.0 copy-start.6
  17.6 8.4 %all-to-all-start = ((bf16[8,64,2048]{2,0,1:T(8,128)(2,1)}), bf16[8,64,2048]{2,0,1:T(8,128)(2,1)S(1)}, u32[]{:S(2)}, u32[]{:S(2)}) async-start(bf16[8,64,2048]{2,0,1:T(8,128)(2,1)} %select_bitcast_fusion), calls=%async_computation | async-start | bytes 4194304 | tf_op jit(solution)/shard_map/all_to_all | solution.py:19
  26.0 0.0 all-reduce.2.cloned.1.call-start
  26.1 0.0 copy-done.6
  26.1 43.0 %all-to-all-done = bf16[8,64,2048]{2,0,1:T(8,128)(2,1)S(1)} async-done(((bf16[8,64,2048]{2,0,1:T(8,128)(2,1)}), bf16[8,64,2048]{2,0,1:T(8,128)(2,1)S(1)}, u32[]{:S(2)}, u32[]{:S(2)}) %all-to-all-start) | async-done | bytes 2097184 | tf_op jit(solution)/shard_map/all_to_all | solution.py:19
  69.1 30.9 %fusion = bf16[128,4,4096]{2,0,1:T(8,128)(2,1)} fusion(f32[4]{0:T(128)S(1)} %convert_element_type.36, bf16[4,4096,2048]{2,1,0:T(8,128)(2,1)} %param.11, bf16[8,16,4,2048]{3,0,2,1:T(8,128)(2,1)S(1)} %bitcast.50), kind=kOutput, calls=%fused_computation.4 | convolution fusion | flops 8594128896 | bytes 73400336 | tf_op jit(solution)/shard_map/psk,sak->psa/dot_general | solution.py:20
  100.0 0.0 all-reduce.2.cloned.1.call-update
  100.0 0.0 all-gather.2.cloned.1.call-start
  100.0 0.5 all-gather.2.cloned.1.call-update
  100.6 32.3 %all-reduce.2.cloned.1.call-done = bf16[128,4,4096]{2,0,1:T(8,128)(2,1)} async-done(((bf16[128,4,4096]{2,0,1:T(8,128)(2,1)}), bf16[128,4,4096]{2,0,1:T(8,128)(2,1)}) %all-reduce.2.cloned.1.call-update) | async-done | bytes 4194320 | tf_op jit(solution)/shard_map/psum | solution.py:25
  132.9 1.7 convert_convert_fusion
  134.6 2.9 %copy.32 = bf16[128,4,2048]{2,1,0:T(4,128)(2,1)} copy(bf16[128,4,2048]{2,0,1:T(8,128)(2,1)S(1)} %convert_convert_fusion) | data formatting | bytes 4194304 | tf_op jit(solution)/shard_map/convert_element_type | solution.py:28
  137.6 0.0 copy-start.1
  137.6 7.0 %all-to-all-start.1 = ((bf16[128,4,2048]{2,1,0:T(4,128)(2,1)}), bf16[128,4,2048]{2,1,0:T(4,128)(2,1)}, u32[]{:S(2)}, u32[]{:S(2)}) async-start(bf16[128,4,2048]{2,1,0:T(4,128)(2,1)} %copy.32), calls=%async_computation.1 | async-start | bytes 4194304 | tf_op jit(solution)/shard_map/all_to_all | solution.py:27
  144.6 0.0 copy-done.1
  144.6 0.0 copy-start.4
  144.6 0.0 slice-start
  144.6 0.0 copy-start.5
  144.6 5.3 %reshape.50 = bf16[8,4,16,32,64]{4,3,0,2,1:T(8,128)(2,1)} reshape(bf16[8,64,2048]{2,0,1:T(8,128)(2,1)S(1)} %copy-done.1) | data formatting | bytes 4194304 | tf_op jit(solution)/shard_map/reshape | solution.py:36
  149.9 0.0 copy-done.4
  149.9 0.1 sub.45
  150.0 0.0 slice-done
  150.0 0.1 slice.15
  150.1 0.1 constant_dynamic-slice_fusion
  150.2 0.0 copy-done.5
  150.2 0.1 broadcast_subtract_fusion
  150.3 4.4 %sub.43 = f32[8,4,16,32,64]{4,3,0,2,1:T(8,128)} broadcast(f32[8,4,32]{2,0,1:T(8,128)S(1)} %broadcast_subtract_fusion), dimensions={0,1,3} | broadcast | bytes 4198400 | tf_op jit(solution)/shard_map/sub | solution.py:52
  154.6 7.8 %sub.44 = f32[8,64,2048]{2,0,1:T(8,128)} reshape(f32[8,4,16,32,64]{4,3,0,2,1:T(8,128)} %sub.43) | data formatting | bytes 8388608 | tf_op jit(solution)/shard_map/sub | solution.py:52
  162.4 9.0 %copy.35 = bf16[8,4,32,16,64]{4,3,2,1,0:T(8,128)(2,1)} copy(bf16[8,4,32,16,64]{4,2,0,3,1:T(8,128)(2,1)} %bitcast.51) | data formatting | bytes 4194304 | tf_op jit(solution)/shard_map/transpose | solution.py:37
  171.4 5.5 %reshape.81 = bf16[8,4,32,1024,1]{3,2,1,0,4:T(8,128)(2,1)S(1)} reshape(bf16[8,4,32,16,64]{4,3,2,1,0:T(8,128)(2,1)} %copy.35) | data formatting | bytes 4194304 | tf_op jit(solution)/shard_map/dot_general | solution.py:40
  176.9 0.1 sub.46
  177.0 1.2 sub.47
  178.2 1.0 scatter_custom_fusion
  179.2 9.2 %all-gather.2.cloned.1.call-done = bf16[1024,1024]{1,0:T(8,128)(2,1)} async-done(((bf16[64,1024]{1,0:T(8,128)(2,1)}), bf16[1024,1024]{1,0:T(8,128)(2,1)}) %all-gather.2.cloned.1.call-update) | async-done | bytes 2097168 | tf_op jit(solution)/shard_map/all_gather | solution.py:42
  188.4 3.9 %copy.36 = bf16[1024,1024]{1,0:T(8,128)(2,1)} copy(bf16[1024,1024]{0,1:T(8,128)(2,1)} %bitcast.53) | data formatting | bytes 4194304 | tf_op jit(solution)/shard_map/dot_general | solution.py:40
  192.3 7.9 %convolution_bitcast_fusion = f32[8,4,16,32,64]{4,3,2,1,0:T(8,128)} fusion(bf16[16,64,1024,1,1]{2,1,0,4,3:T(8,128)(2,1)} %bitcast.54, bf16[8,4,32,1024,1]{3,2,1,0,4:T(8,128)(2,1)S(1)} %reshape.81), kind=kOutput, calls=%fused_computation.11 | convolution fusion | flops 2147483648 | bytes 8388608 | tf_op jit(solution)/shard_map/dot_general | solution.py:40
  200.2 7.8 %reshape.51 = f32[8,64,2048]{2,1,0:T(8,128)} reshape(f32[8,4,16,32,64]{4,3,2,1,0:T(8,128)} %convolution_bitcast_fusion) | data formatting | bytes 8388608 | tf_op jit(solution)/shard_map/reshape | solution.py:46
  208.0 0.0 all-to-all-done.1
  208.0 2.8 %convert_bitcast_fusion = f32[8,16,4,2048]{3,0,1,2:T(8,128)S(1)} fusion(bf16[128,4,2048]{2,1,0:T(4,128)(2,1)} %all-to-all-done.1), kind=kLoop, calls=%fused_computation.5 | loop fusion | flops 1048576 | bytes 6291456 | tf_op jit(solution)/shard_map/convert_element_type | solution.py:29
  210.8 2.2 copy.34
  213.1 0.0 copy-start.2
  213.1 0.0 copy-start.3
  213.1 5.1 %gather_fusion.1 = f32[64,8,2048]{2,1,0:T(8,128)} fusion(f32[8,64,2048]{2,0,1:T(8,128)} %bitcast.52, s32[1024]{0:T(1024)S(1)} %pad_clamp_fusion), kind=kCustom, calls=%fused_computation.1 | custom fusion | bytes 8388864 | tf_op jit(solution)/shard_map/jit(_take)/gather | solution.py:35
  218.2 0.0 copy-done.2
  218.2 0.0 copy-done.3
  218.2 10.3 %fusion.3 = bf16[8,64,2048]{2,0,1:T(8,128)(2,1)S(1)} fusion(f32[8,64,2048]{2,1,0:T(8,128)} %reshape.51, f32[64,8,2048]{2,1,0:T(8,128)} %gather_fusion.1, f32[8,64,2048]{2,0,1:T(8,128)} %sub.44, f32[64,2048]{1,0:T(8,128)S(1)} %copy-done.3, pred[64]{0:T(512)(128)(4,1)S(1)} %compare_and_fusion.1, bf16[8,64,2048]{2,1,0:T(8,128)(2,1)S(1)} %copy-done.2, ...), kind=kLoop, calls=%fused_computation.9 | loop fusion | flops 8388608 | bytes 17302080 | tf_op jit(solution)/shard_map/convert_element_type | solution.py:58
  228.5 2.5 %copy.38 = bf16[8,64,2048]{2,1,0:T(8,128)(2,1)} copy(bf16[8,64,2048]{2,0,1:T(8,128)(2,1)S(1)} %fusion.3) | data formatting | bytes 4194304 | tf_op jit(solution)/shard_map/convert_element_type | solution.py:58
  (6 shorter events, 0.0 us)
Async XLA Ops:
  12.4 2.0 copy-start
  17.6 8.5 %copy-start.6 = (s32[4]{0:T(128)S(1)}, s32[4]{0:T(128)}, u32[]{:S(2)}) copy-start(s32[4]{0:T(128)} %param.12) | copy-start | bytes 52
  17.6 51.5 %all-to-all-start = ((bf16[8,64,2048]{2,0,1:T(8,128)(2,1)}), bf16[8,64,2048]{2,0,1:T(8,128)(2,1)S(1)}, u32[]{:S(2)}, u32[]{:S(2)}) async-start(bf16[8,64,2048]{2,0,1:T(8,128)(2,1)} %select_bitcast_fusion), calls=%async_computation | async-start | bytes 4194304 | tf_op jit(solution)/shard_map/all_to_all | solution.py:19
  26.0 106.9 %all-reduce.2.cloned.1.call-start = ((), (), s32[]{:S(2)}) async-start(), calls=%async_computation.2 | async-start | bytes 8388608 | tf_op jit(solution)/shard_map/psum | solution.py:25
  100.0 88.4 %all-gather.2.cloned.1.call-start = ((), (), s32[]{:S(2)}) async-start(), calls=%async_computation.3 | async-start | bytes 2228224 | tf_op jit(solution)/shard_map/all_gather | solution.py:42
  137.6 7.0 %copy-start.1 = (bf16[8,64,2048]{2,0,1:T(8,128)(2,1)S(1)}, bf16[8,64,2048]{2,0,1:T(8,128)(2,1)}, u32[]{:S(2)}) copy-start(bf16[8,64,2048]{2,0,1:T(8,128)(2,1)} %copy-done) | copy-start | bytes 6291460
  137.6 70.4 %all-to-all-start.1 = ((bf16[128,4,2048]{2,1,0:T(4,128)(2,1)}), bf16[128,4,2048]{2,1,0:T(4,128)(2,1)}, u32[]{:S(2)}, u32[]{:S(2)}) async-start(bf16[128,4,2048]{2,1,0:T(4,128)(2,1)} %copy.32), calls=%async_computation.1 | async-start | bytes 4194304 | tf_op jit(solution)/shard_map/all_to_all | solution.py:27
  144.6 5.4 %copy-start.4 = (f32[1024]{0:T(1024)S(1)}, f32[1024]{0:T(1024)}, u32[]{:S(2)}) copy-start(f32[1024]{0:T(1024)} %param.15) | copy-start | bytes 12292
  144.6 5.4 %slice-start = ((f32[1024]{0:T(1024)}), f32[256]{0:T(256)S(1)}, s32[]{:S(2)}) async-start(f32[1024]{0:T(1024)} %param.15), calls=%async_computation.4 | async-start | bytes 2048 | tf_op jit(solution)/shard_map/slice | solution.py:50
  144.6 5.6 %copy-start.5 = (f32[8]{0:T(128)S(1)}, f32[8]{0:T(128)}, u32[]{:S(2)}) copy-start(f32[8]{0:T(128)} %param.16) | copy-start | bytes 100
  213.1 5.1 %copy-start.2 = (bf16[8,64,2048]{2,1,0:T(8,128)(2,1)S(1)}, bf16[8,64,2048]{2,1,0:T(8,128)(2,1)}, u32[]{:S(2)}) copy-start(bf16[8,64,2048]{2,1,0:T(8,128)(2,1)} %param.9) | copy-start | bytes 6291460
  213.1 5.1 %copy-start.3 = (f32[64,2048]{1,0:T(8,128)S(1)}, f32[64,2048]{1,0:T(8,128)}, u32[]{:S(2)}) copy-start(f32[64,2048]{1,0:T(8,128)} %sub.47) | copy-start | bytes 1572868
Sparse Core Ops, SparseCore 0:
  100.1 32.7 all-reduce.1
Sparse Core Ops, SparseCore 1:
  103.2 85.1 all-gather.1
where the time goes:
time: 240 us; the launch traced here: 238 us
  waiting for transfers between devices  85 us (35%)
  local copies, waits for them, and re-layouts  61.1 us (25%)
  matrix products  38.8 us (16%)
  other arithmetic  23 us (10%)
  starting transfers between devices  15.5 us (6%)
  between operations  15 us (6%)
    all_to_all x1, waiting for transfers between devices, shards(): lax.all_to_all(ordered, 'pair', split_axis=1, concat_axis=0, tiled=True)  43 us
    psum x1, waiting for transfers between devices, shards(): lax.psum(partial_value.astype(jnp.bfloat16), 'int').astype(jnp.float32)  32.3 us
    dot_general x1, matrix products, shards(): jnp.einsum('psk,sak->psa', received, integrals, preferred_element_type=jn...  30.9 us
    sub x5, local copies, waits for them, and re-layouts, shards(): pair_energy[:, None, None, None, None] - own_energy[None, :, None, :, None]  13.5 us
    convert_element_type x1, other arithmetic, shards(): return updated.astype(jnp.bfloat16)  10.3 us
    dot_general x2, local copies, waits for them, and re-layouts, shards(): jnp.dot(tile_rows, lax.all_gather(dressing, 'pair', axis=0, tiled=True),...  9.41 us
    all_gather x1, waiting for transfers between devices, shards(): lax.all_gather(dressing, 'pair', axis=0, tiled=True)  9.16 us
    transpose x1, local copies, waits for them, and re-layouts, shards(): jnp.transpose(tile_rows, (0, 1, 3, 2, 4))  9 us
  transfers between devices with their start and end apart: 4, of which 3 were waited for; matrix products, arithmetic and copies ran while one was open for 25% of the time, Pallas kernels for 0%

commit v1 on v0

v1 whole, which is shorter than its diff:
```python
import jax
import jax.numpy as jnp
from jax import lax
from jax.experimental import pallas as pl
from jax.experimental.pallas import tpu as pltpu
from jax.sharding import PartitionSpec as P

TILE = 64
VT = 16
WA = 4
LANES = 128
MIB = 1 << 20


def prepare_kernel(owners, in_tiles_ref, amps_ref, mask_ref, tiles_ref, *sent_refs):
    tile_count = amps_ref.shape[1]
    swapped = jnp.swapaxes(amps_ref[...].astype(jnp.float32), 0, 1)
    for tile in range(tile_count):
        kept = jnp.where(mask_ref[:, tile : tile + 1] > 0, swapped[tile], 0.0)
        tiles_ref[tile] = kept.astype(tiles_ref.dtype)
    size = tile_count // owners // len(sent_refs)
    for chunk, sent_ref in enumerate(sent_refs):
        for owner in range(owners):
            for slot in range(size):
                source = in_tiles_ref[(owner * len(sent_refs) + chunk) * size + slot]
                sent_ref[owner, slot] = tiles_ref[source]


def prepare(in_tiles, amps, amp_mask, owners, chunks):
    pairs, tiles, share = amps.shape
    width = min(share, 1024)
    size = tiles // owners // chunks
    return pl.pallas_call(
        lambda *refs: prepare_kernel(owners, *refs),
        out_shape=(jax.ShapeDtypeStruct((tiles, pairs, share), amps.dtype),)
        + (jax.ShapeDtypeStruct((owners, size, pairs, share), amps.dtype),) * chunks,
        grid_spec=pltpu.PrefetchScalarGridSpec(
            num_scalar_prefetch=1,
            grid=(share // width,),
            in_specs=[
                pl.BlockSpec((pairs, tiles, width), lambda i, _: (0, 0, i)),
                pl.BlockSpec((pairs, tiles), lambda i, _: (0, 0)),
            ],
            out_specs=[pl.BlockSpec((tiles, pairs, width), lambda i, _: (0, 0, i))]
            + [pl.BlockSpec((owners, size, pairs, width), lambda i, _: (0, 0, 0, i))] * chunks,
        ),
        compiler_params=pltpu.CompilerParams(vmem_limit_bytes=56 * MIB),
        cost_estimate=pl.CostEstimate(
            flops=2 * pairs * tiles * share,
            bytes_accessed=6 * pairs * tiles * share,
            transcendentals=0,
        ),
    )(in_tiles, amps, amp_mask)


def ladder_kernel(first_slot, index_ref, keep_ref, x_ref, w_ref, *rest):
    out_refs, x_rows = rest[:-1], rest[-1]
    part, slot, block = pl.program_id(0), pl.program_id(1), pl.program_id(2)
    rows, depth = x_rows.shape

    @pl.when(block == 0)
    def _():
        x = x_ref[:, 0].astype(jnp.float32).reshape(rows, depth)
        x_rows[...] = x.astype(x_rows.dtype)

    keep = keep_ref[first_slot + slot] > 0
    product = lax.dot_general(
        x_rows[...], w_ref[0], (((1,), (1,)), ((), ())), preferred_element_type=jnp.float32
    )
    product = jnp.where(keep, product, 0.0)
    for index, out_ref in enumerate(out_refs):

        @pl.when(part == index)
        def _():
            shape = (out_ref.shape[0], out_ref.shape[2], out_ref.shape[3])
            out_ref[:, 0] = product.reshape(shape).astype(out_ref.dtype)


def ladder(int_index, block_mask, received, integrals, chunk, parts):
    owners, chunk_slots, pairs, depth = received.shape
    entries = integrals.shape[1]
    share = entries // parts
    width = min(share, 2048)
    blocks = share // width
    first_slot = chunk * chunk_slots

    def block_of(part, block, index_ref):
        return lax.rem(index_ref[0] + 1 + part, parts) * blocks + block

    def out_map(index):
        def where(part, slot, block, index_ref, keep_ref):
            at = lambda value, last: jnp.where(
                part == index, value, jnp.where(part < index, 0, last)
            )
            return (0, at(slot, chunk_slots - 1), 0, at(block, blocks - 1))

        return where

    return pl.pallas_call(
        lambda *refs: ladder_kernel(first_slot, *refs),
        out_shape=tuple(
            jax.ShapeDtypeStruct((owners, chunk_slots, pairs, share), received.dtype)
            for _ in range(parts)
        ),
        grid_spec=pltpu.PrefetchScalarGridSpec(
            num_scalar_prefetch=2,
            grid=(parts, chunk_slots, blocks),
            in_specs=[
                pl.BlockSpec((owners, 1, pairs, depth), lambda h, s, b, i, k: (0, s, 0, 0)),
                pl.BlockSpec(
                    (1, width, depth), lambda h, s, b, i, k: (first_slot + s, block_of(h, b, i), 0)
                ),
            ],
            out_specs=[
                pl.BlockSpec((owners, 1, pairs, width), out_map(index)) for index in range(parts)
            ],
            scratch_shapes=[pltpu.VMEM((owners * pairs, depth), received.dtype)],
        ),
        compiler_params=pltpu.CompilerParams(vmem_limit_bytes=24 * MIB),
        cost_estimate=pl.CostEstimate(
            flops=2 * owners * pairs * chunk_slots * entries * depth,
            bytes_accessed=2 * chunk_slots * entries * depth,
            transcendentals=0,
        ),
    )(int_index, block_mask, received, integrals)


def cycle_kernel(
    owners, parts, place_ref, tiles_ref, first_ref, second_ref, energy_ref, *rest
):
    pieces, (base_ref, dress, wide, rows) = rest[:-4], rest[-4:]
    groups = tiles_ref.shape[2] // LANES
    pairs = tiles_ref.shape[1]
    outer_tile = pl.program_id(0)

    @pl.when(outer_tile == 0)
    def _():
        own = pieces[0].shape[2]
        for owner in range(owners):
            for part in range(parts):
                away = place_ref[1] ^ part
                source = place_ref[0] ^ owner
                block = pieces[0][lax.div(away, len(pieces)), source].astype(jnp.float32)
                for index in range(1, len(pieces)):
                    other = pieces[index][lax.div(away, len(pieces)), source].astype(jnp.float32)
                    block = jnp.where(lax.rem(away, len(pieces)) == index, other, block)
                start = (owner * parts + part) * own
                dress[start : start + own] = block
        low = lax.broadcasted_iota(jnp.int32, (TILE, LANES), 1) < TILE
        for inner in range(VT):
            for couple in range(VT // 2):
                block = dress[
                    inner * TILE : (inner + 1) * TILE, couple * LANES : (couple + 1) * LANES
                ]
                turned = pltpu.roll(block, TILE, 1)
                even = slice(2 * couple * LANES, (2 * couple + 1) * LANES)
                odd = slice((2 * couple + 1) * LANES, (2 * couple + 2) * LANES)
                upper = slice(inner * LANES, inner * LANES + TILE)
                lower = slice(inner * LANES + TILE, (inner + 1) * LANES)
                wide[upper, even] = jnp.where(low, block, 0.0).astype(wide.dtype)
                wide[upper, odd] = jnp.where(low, turned, 0.0).astype(wide.dtype)
                wide[lower, even] = jnp.where(low, 0.0, turned).astype(wide.dtype)
                wide[lower, odd] = jnp.where(low, 0.0, block).astype(wide.dtype)

    for inner in range(VT):
        tile = tiles_ref[inner].astype(jnp.float32)
        stacked = jnp.concatenate(
            [tile[:, g * LANES : (g + 1) * LANES] for g in range(groups)], axis=0
        )
        rows[:, inner * LANES : (inner + 1) * LANES] = stacked.astype(rows.dtype)
    for outer in range(0, VT, 2):
        span = slice(outer * LANES, (outer + 2) * LANES)
        product = jnp.dot(rows[...], wide[:, span], preferred_element_type=jnp.float32)
        for half in range(2):
            cycle = jnp.concatenate(
                [
                    product[g * pairs : (g + 1) * pairs, half * LANES : (half + 1) * LANES]
                    for g in range(groups)
                ],
                axis=1,
            )
            b = outer + half
            below = energy_ref[...] - first_ref[0] - second_ref[b]
            base_ref[b] = tiles_ref[b].astype(jnp.float32) + cycle / below


def cycle_terms(place, tiles, first, second, pair_energy, pieces, owners, parts):
    count, pairs, share = tiles.shape
    whole = lambda a: pl.BlockSpec(a.shape, lambda i, *_: (0,) * a.ndim)
    return pl.pallas_call(
        lambda *refs: cycle_kernel(owners, parts, *refs),
        out_shape=jax.ShapeDtypeStruct(tiles.shape, jnp.float32),
        grid_spec=pltpu.PrefetchScalarGridSpec(
            num_scalar_prefetch=1,
            grid=(WA,),
            in_specs=[
                pl.BlockSpec((VT, pairs, share), lambda i, *_: (i, 0, 0)),
                pl.BlockSpec((1, 1, share), lambda i, *_: (i, 0, 0)),
                whole(second),
                whole(pair_energy),
            ]
            + [whole(piece) for piece in pieces],
            out_specs=pl.BlockSpec((VT, pairs, share), lambda i, *_: (i, 0, 0)),
            scratch_shapes=[
                pltpu.VMEM((VT * TILE, VT * TILE), jnp.float32),
                pltpu.VMEM((VT * LANES, VT * LANES), tiles.dtype),
                pltpu.VMEM((pairs * share // LANES, VT * LANES), tiles.dtype),
            ],
        ),
        compiler_params=pltpu.CompilerParams(vmem_limit_bytes=48 * MIB),
        cost_estimate=pl.CostEstimate(
            flops=4 * count * pairs * share * VT * TILE,
            bytes_accessed=8 * count * pairs * share,
            transcendentals=0,
        ),
    )(place, tiles, first, second, pair_energy, *pieces)


def finish_kernel(
    chunks, out_tiles_ref, base_ref, first_ref, second_ref, energy_ref, *rest
):
    parts, out_ref, sums = rest[:chunks], rest[-2], rest[-1]
    for chunk, part in enumerate(parts):
        owners, size = part.shape[:2]
        for owner in range(owners):
            for slot in range(size):
                tile = out_tiles_ref[(owner * chunks + chunk) * size + slot]
                below = (
                    energy_ref[...] - first_ref[lax.div(tile, VT)] - second_ref[lax.rem(tile, VT)]
                )
                sums[tile] = base_ref[tile] + part[owner, slot].astype(jnp.float32) / below
    out_ref[...] = jnp.swapaxes(sums[...], 0, 1).astype(out_ref.dtype)


def finish(out_tiles, base, first, second, pair_energy, parts, dtype):
    count, pairs, share = base.shape
    width = min(share, 512)
    return pl.pallas_call(
        lambda *refs: finish_kernel(len(parts), *refs),
        out_shape=jax.ShapeDtypeStruct((pairs, count, share), dtype),
        grid_spec=pltpu.PrefetchScalarGridSpec(
            num_scalar_prefetch=1,
            grid=(share // width,),
            in_specs=[
                pl.BlockSpec((count, pairs, width), lambda i, _: (0, 0, i)),
                pl.BlockSpec((WA, 1, width), lambda i, _: (0, 0, i)),
                pl.BlockSpec((VT, 1, width), lambda i, _: (0, 0, i)),
                pl.BlockSpec((pairs, 1), lambda i, _: (0, 0)),
            ]
            + [
                pl.BlockSpec(part.shape[:2] + (pairs, width), lambda i, _: (0, 0, 0, i))
                for part in parts
            ],
            out_specs=pl.BlockSpec((pairs, count, width), lambda i, _: (0, 0, i)),
            scratch_shapes=[pltpu.VMEM((count, pairs, width), jnp.float32)],
        ),
        compiler_params=pltpu.CompilerParams(vmem_limit_bytes=56 * MIB),
        cost_estimate=pl.CostEstimate(
            flops=8 * count * pairs * share,
            bytes_accessed=8 * count * pairs * share,
            transcendentals=0,
        ),
    )(out_tiles, base, first, second, pair_energy, *parts)


def exchanges(axis, size, radices):
    steps, reach = [], size
    while reach > 1:
        radix = radices.pop(0) if radices else 4
        radix = radix if reach % radix == 0 else 2
        reach //= radix
        steps.append((axis, size, [reach * m for m in range(1, radix)]))
    return steps


def exchange(block, step):
    axis, size, distances = step
    others = [
        lax.ppermute(block, axis, [(j, j ^ distance) for j in range(size)])
        for distance in distances
    ]
    return [block, *others]


def joined(blocks):
    return jnp.stack(blocks, axis=1).reshape((-1,) + blocks[0].shape[1:])


def solution(mesh):
    owners, parts = mesh.shape["pair"], mesh.shape["int"]

    def shards(
        amps, amp_mask, integrals, block_mask, in_tiles, out_tiles, vir_energy, pair_energy, dressing
    ):
        pairs, tiles, share = amps.shape
        slots = tiles // owners
        chunks = 2 if slots % 2 == 0 else 1
        size = slots // chunks
        strip = share // TILE
        int_index = lax.axis_index("int")

        masked, *sent = prepare(in_tiles, amps, amp_mask, owners, chunks)

        def exchanged(part):
            return lax.all_to_all(part, "pair", split_axis=0, concat_axis=0, tiled=True)

        rows, columns = dressing.shape
        own = rows // parts
        steps = exchanges("pair", owners, [2, 2])
        gathered = [lax.dynamic_slice_in_dim(dressing, int_index * own, own, 0)[None]]
        together = lax.optimization_barrier
        received, returned = [], []
        for c in range(chunks):
            if c:
                received[-1], sent[c] = together((received[-1], sent[c]))
            received.append(exchanged(sent[c]))
        for c in range(chunks):
            if c == 0 and steps:
                gathered = exchange(joined(gathered), steps.pop(0))
            if c == 0:
                received[c], gathered = together((received[c], gathered))
            if steps:
                gathered = exchange(joined(gathered), steps.pop(0))
            terms = ladder(
                int_index.astype(jnp.int32)[None], block_mask, received[c], integrals, c, parts
            )
            (*others, total), gathered = together((terms, gathered))
            total = total.astype(jnp.float32)
            for r, other in enumerate(others):
                got = lax.ppermute(
                    other, "int", [(j, (j + 1 + r) % parts) for j in range(parts)]
                )
                total = total + got.astype(jnp.float32)
            total = total.astype(amps.dtype)
            if c == 0:
                received[-1], total = together((received[-1], total))
            else:
                returned[-1], total = together((returned[-1], total))
            returned.append(exchanged(total))

        while steps:
            gathered = exchange(joined(gathered), steps.pop(0))
        returned[0], gathered = together((returned[0], gathered))
        pieces = [joined(gathered)[None]]
        for step in exchanges("int", parts, []):
            pieces = exchange(joined(pieces), step)

        energies = vir_energy.reshape(VT, TILE)
        own_energy = lax.dynamic_slice_in_dim(energies[:WA], int_index * strip, strip, 1)
        first = jnp.repeat(own_energy, TILE, axis=1)[:, None]
        second = jnp.tile(energies, (1, strip))[:, None]
        energy = pair_energy[:, None]
        place = jnp.stack([lax.axis_index("pair"), int_index]).astype(jnp.int32)
        base = cycle_terms(place, masked, first, second, energy, pieces, owners, parts)
        return finish(out_tiles, base, first, second, energy, returned, amps.dtype)

    in_specs = (
        P("pair", None, "int"),
        P("pair", None),
        P("pair", None, "int"),
        P("pair"),
        P(),
        P(),
        P(),
        P("pair"),
        P("pair", None),
    )
    out_specs = P("pair", None, "int")
    return jax.shard_map(shards, mesh=mesh, in_specs=in_specs, out_specs=out_specs, check_vma=False)
```

time: 240 us -> 139 us (0.58)
  local copies, waits for them, and re-layouts: 61.1 us -> 2.39 us
  Pallas kernels: 0 us -> 54.5 us
  waiting for transfers between devices: 85 us -> 41.5 us
  matrix products: 38.8 us -> 0 us
  starting transfers between devices: 15.5 us -> 35.6 us
  other arithmetic: 23 us -> 4.1 us
  between operations: 15 us -> 0.22 us
    pallas_call x0 -> x5, Pallas kernels: none -> 54.5 us  [the longest x2 33.1 us: ladder(): pl.pallas_call(lambda *refs: ladder_kernel(first_slot, *refs), out_shape=...]
    dot_general x2 -> x0, matrix products: 38.8 us -> none  [the longest x1 30.9 us: shards(): jnp.einsum('psk,sak->psa', received, integrals, preferred_element_type=jn...]
    psum x1 -> x0, waiting for transfers between devices: 32.3 us -> none  [shards(): lax.psum(partial_value.astype(jnp.bfloat16), 'int').astype(jnp.float32)]
    sub x5 -> x0, local copies, waits for them, and re-layouts: 13.5 us -> none  [shards(): pair_energy[:, None, None, None, None] - own_energy[None, :, None, :, None]]
    reshape x2 -> x0, local copies, waits for them, and re-layouts: 13.2 us -> none  [the longest x1 7.83 us: shards(): jnp.transpose(running, (0, 1, 3, 2, 4))]
    convert_element_type x4 -> x2, other arithmetic: 14.9 us -> 2.74 us  [shards(): total = total.astype(amps.dtype)]
    all_to_all x2 -> x4, starting transfers between devices: 15.4 us -> 27 us  [exchanged(): return lax.all_to_all(part, 'pair', split_axis=0, concat_axis=0, tiled=True)]
    dot_general x2 -> x0, local copies, waits for them, and re-layouts: 9.41 us -> none  [shards(): jnp.dot(tile_rows, lax.all_gather(dressing, 'pair', axis=0, tiled=True),...]
  transfers between devices with their start and end apart: 4 -> 12, of which waited for: 3 -> 7; matrix products, arithmetic and copies ran while one was open for 25% -> 5% of each run, Pallas kernels for 0% -> 31%
where the time goes in v1:
time: 139 us; the launch traced here: 138 us
  Pallas kernels  54.5 us (39%)
  waiting for transfers between devices  41.5 us (30%)
  starting transfers between devices  35.6 us (26%)
  other arithmetic  4.1 us (3%)
  local copies, waits for them, and re-layouts  2.39 us (2%)
    all_to_all x4, waiting for transfers between devices, exchanged(): return lax.all_to_all(part, 'pair', split_axis=0, concat_axis=0, tiled=True)  35.3 us
    pallas_call x2, Pallas kernels, ladder(): pl.pallas_call(lambda *refs: ladder_kernel(first_slot, *refs), out_shape=...  33.1 us
    all_to_all x4, starting transfers between devices, exchanged(): return lax.all_to_all(part, 'pair', split_axis=0, concat_axis=0, tiled=True)  27 us
    pallas_call x1, Pallas kernels, cycle_terms(): pl.pallas_call(lambda *refs: cycle_kernel(owners, parts, *refs), out_shap...  10 us
    ppermute x6, starting transfers between devices, exchange(): lax.ppermute(block, axis, [(j, j ^ distance) for j in range(size)])  8.5 us
    pallas_call x1, Pallas kernels, finish(): pl.pallas_call(lambda *refs: finish_kernel(len(parts), *refs), out_shape=...  6.69 us
    pallas_call x1, Pallas kernels, prepare(): pl.pallas_call(lambda *refs: prepare_kernel(owners, *refs), out_shape=(ja...  4.7 us
    ppermute x6, waiting for transfers between devices, exchange(): lax.ppermute(block, axis, [(j, j ^ distance) for j in range(size)])  3.55 us
  transfers between devices with their start and end apart: 12, of which 7 were waited for; matrix products, arithmetic and copies ran while one was open for 5% of the time, Pallas kernels for 31%

profile of v1, /device:TPU:0, one launch (start us, length us, event | category | flops | bytes accessed | tf_op | source)
XLA Modules:
  0.0 138.3 jit_solution(6078355093734279546)
XLA Ops:
  0.0 0.0 copy-start
  0.0 4.7 %shard_map.91 = (bf16[64,8,2048]{2,1,0:T(8,128)(2,1)}, bf16[16,2,8,2048]{3,2,1,0:T(8,128)(2,1)}, bf16[16,2,8,2048]{3,2,1,0:T(8,128)(2,1)}) custom-call(s32[64]{0:T(128)} %refs_0_.2, bf16[8,64,2048]{2,1,0:T(8,128)(2,1)} %refs_1_.3, s32[8,64]{1,0:T(8,128)} %refs_2_.1), custom_call_target="tpu_custom_call" | custom-call | flops 2097152 | bytes 6291456 | tf_op jit(solution)/shard_map/pallas_call | solution.py:33
  4.7 0.0 copy-start.4
  4.7 8.4 %all-to-all-start = ((bf16[16,2,8,2048]{3,2,1,0:T(8,128)(2,1)}), bf16[16,2,8,2048]{3,2,1,0:T(8,128)(2,1)S(1)}, u32[]{:S(2)}, u32[]{:S(2)}) async-start(bf16[16,2,8,2048]{3,2,1,0:T(8,128)(2,1)} %get-tuple-element.37), calls=%async_computation | async-start | bytes 2097152 | tf_op jit(solution)/shard_map/all_to_all | solution.py:305
  13.2 0.0 copy-done
  13.2 2.9 %collective-permute-start = (bf16[1,32,1024]{2,1,0:T(8,128)(2,1)S(1)}, bf16[1,32,1024]{2,1,0:T(8,128)(2,1)S(1)}, u32[]{:S(2)}, u32[]{:S(2)}) collective-permute-start(bf16[1,32,1024]{2,1,0:T(8,128)(2,1)S(1)} %dynamic-slice_bitcast_fusion), channel_id=1, source_target_pairs={{0,16},{2,18},{4,20},{6,22},{8,24},{10,26},{12,28},{14,30},{16,0},... | collective-permute-start | bytes 196616 | tf_op jit(solution)/shard_map/ppermute | solution.py:279
  16.1 22.9 %all-to-all-done.refs_2_ = bf16[16,2,8,2048]{3,2,1,0:T(8,128)(2,1)S(1)} async-done(((bf16[16,2,8,2048]{3,2,1,0:T(8,128)(2,1)}), bf16[16,2,8,2048]{3,2,1,0:T(8,128)(2,1)S(1)}, u32[]{:S(2)}, u32[]{:S(2)}) %all-to-all-start) | async-done | bytes 1048608 | tf_op jit(solution)/shard_map/all_to_all | solution.py:305
  39.0 2.6 %collective-permute-done = bf16[1,32,1024]{2,1,0:T(8,128)(2,1)S(1)} collective-permute-done((bf16[1,32,1024]{2,1,0:T(8,128)(2,1)S(1)}, bf16[1,32,1024]{2,1,0:T(8,128)(2,1)S(1)}, u32[]{:S(2)}, u32[]{:S(2)}) %collective-permute-start) | collective-permute-done | bytes 65568 | tf_op jit(solution)/shard_map/ppermute | solution.py:279
  41.6 4.6 %all-to-all-start.1 = ((bf16[16,2,8,2048]{3,2,1,0:T(8,128)(2,1)}), bf16[16,2,8,2048]{3,2,1,0:T(8,128)(2,1)S(1)}, u32[]{:S(2)}, u32[]{:S(2)}) async-start(bf16[16,2,8,2048]{3,2,1,0:T(8,128)(2,1)} %get-tuple-element.39), calls=%async_computation.1 | async-start | bytes 2097152 | tf_op jit(solution)/shard_map/all_to_all | solution.py:305
  46.3 2.0 %collective-permute-start.1 = (bf16[2,32,1024]{2,1,0:T(8,128)(2,1)S(1)}, bf16[2,32,1024]{2,1,0:T(8,128)(2,1)S(1)}, u32[]{:S(2)}, u32[]{:S(2)}) collective-permute-start(bf16[2,32,1024]{2,1,0:T(8,128)(2,1)S(1)} %maximum_bitcast_fusion), channel_id=1, source_target_pairs={{0,8},{2,10},{4,12},{6,14},{8,0},{10,2},{12,4},{14,6},{16,24},{18,... | collective-permute-start | bytes 393224 | tf_op jit(solution)/shard_map/ppermute | solution.py:279
  48.2 0.0 copy-done.4
  48.2 16.5 %shard_map.92 = (bf16[16,2,8,2048]{3,2,1,0:T(8,128)(2,1)S(1)}, bf16[16,2,8,2048]{3,2,1,0:T(8,128)(2,1)S(1)}) custom-call(s32[1]{0:T(128)} %bitcast.1.refs_0_, s32[4]{0:T(128)S(1)} %copy-done.4, bf16[16,2,8,2048]{3,2,1,0:T(8,128)(2,1)S(1)} %all-to-all-done.refs_2_, bf16[4,4096,2048]{2,1,0:T(8,128)(2,1)} %refs_3_.3), custom_call_target="tpu_custom_call" | custom-call | flops 4294967296 | bytes 33554432 | tf_op jit(solution)/shard_map/pallas_call | solution.py:99
  64.8 0.6 collective-permute-done.1
  65.4 0.0 collective-permute-start.2
  65.4 2.7 %collective-permute-start.5 = (bf16[4,32,1024]{2,1,0:T(8,128)(2,1)S(1)}, bf16[4,32,1024]{2,1,0:T(8,128)(2,1)S(1)}, u32[]{:S(2)}, u32[]{:S(2)}) collective-permute-start(bf16[4,32,1024]{2,1,0:T(8,128)(2,1)S(1)} %bitcast.27), channel_id=1, source_target_pairs={{0,6},{2,4},{4,2},{6,0},{8,14},{10,12},{12,10},{14,8},{16,22},{18,... | collective-permute-start | bytes 786440 | tf_op jit(solution)/shard_map/ppermute | solution.py:279
  68.2 0.5 collective-permute-start.4
  68.7 0.3 collective-permute-start.3
  69.0 0.0 collective-permute-done.2
  69.0 1.4 add_convert_fusion.1
  70.4 0.0 all-to-all-done.1.refs_2_
  70.4 8.0 %all-to-all-start.2 = ((bf16[16,2,8,2048]{3,2,1,0:T(8,128)(2,1)}), bf16[16,2,8,2048]{3,2,1,0:T(8,128)(2,1)}, u32[]{:S(2)}, u32[]{:S(2)}) async-start(bf16[16,2,8,2048]{3,2,1,0:T(8,128)(2,1)} %add_convert_fusion.1), calls=%async_computation.2 | async-start | bytes 2097152 | tf_op jit(solution)/shard_map/all_to_all | solution.py:305
  78.3 16.5 %shard_map.93 = (bf16[16,2,8,2048]{3,2,1,0:T(8,128)(2,1)S(1)}, bf16[16,2,8,2048]{3,2,1,0:T(8,128)(2,1)S(1)}) custom-call(s32[1]{0:T(128)} %bitcast.1.refs_0_, s32[4]{0:T(128)S(1)} %copy-done.4, bf16[16,2,8,2048]{3,2,1,0:T(8,128)(2,1)S(1)} %all-to-all-done.1.refs_2_, bf16[4,4096,2048]{2,1,0:T(8,128)(2,1)} %refs_3_.3), custom_call_target="tpu_custom_call" | custom-call | flops 4294967296 | bytes 33554432 | tf_op jit(solution)/shard_map/pallas_call | solution.py:99
  94.9 0.0 collective-permute-done.5
  94.9 0.0 copy-start.6
  94.9 0.0 collective-permute-done.4
  94.9 0.0 copy-start.7
  94.9 0.0 collective-permute-done.3
  94.9 0.0 copy-start.8
  95.0 0.1 collective-permute-start.6
  95.0 2.6 %collective-permute-done.6 = bf16[16,2,8,2048]{3,2,1,0:T(8,128)(2,1)S(1)} collective-permute-done((bf16[16,2,8,2048]{3,2,1,0:T(8,128)(2,1)S(1)}, bf16[16,2,8,2048]{3,2,1,0:T(8,128)(2,1)S(1)}, u32[]{:S(2)}, u32[]{:S(2)}) %collective-permute-start.6) | collective-permute-done | bytes 1048608 | tf_op jit(solution)/shard_map/ppermute | solution.py:330
  97.7 1.4 add_convert_fusion
  99.0 0.0 copy-start.9
  99.0 0.0 slice-start
  99.0 0.0 copy-start.10
  99.0 0.0 copy-start.5
  99.1 3.5 %all-to-all-done.2.refs_5_ = bf16[16,2,8,2048]{3,2,1,0:T(8,128)(2,1)} async-done(((bf16[16,2,8,2048]{3,2,1,0:T(8,128)(2,1)}), bf16[16,2,8,2048]{3,2,1,0:T(8,128)(2,1)}, u32[]{:S(2)}, u32[]{:S(2)}) %all-to-all-start.2) | async-done | bytes 1048608 | tf_op jit(solution)/shard_map/all_to_all | solution.py:305
  102.6 0.0 copy-done.6
  102.6 0.0 copy-done.7
  102.6 0.0 copy-done.8
  102.6 6.0 %all-to-all-start.3 = ((bf16[16,2,8,2048]{3,2,1,0:T(8,128)(2,1)}), bf16[16,2,8,2048]{3,2,1,0:T(8,128)(2,1)}, u32[]{:S(2)}, u32[]{:S(2)}) async-start(bf16[16,2,8,2048]{3,2,1,0:T(8,128)(2,1)} %add_convert_fusion), calls=%async_computation.3 | async-start | bytes 2097152 | tf_op jit(solution)/shard_map/all_to_all | solution.py:305
  108.6 1.2 pad_maximum_fusion
  109.8 0.1 collective-permute-start.7
  109.9 0.0 copy-done.9
  109.9 0.1 tile.9
  110.0 0.0 slice-done
  110.0 0.1 slice.15
  110.1 0.0 copy-done.10
  110.1 0.1 copy.14.refs_4_
  110.2 0.1 constant_dynamic-slice_fusion
  110.2 0.1 broadcast_in_dim.11
  110.3 0.1 broadcast_in_dim_reshape.6.refs_2_
  110.4 0.0 copy-start.2
  110.4 0.7 tile.10
  111.2 1.1 tile.11.refs_3_
  112.3 0.0 copy-start.1
  112.3 0.1 pad_add_fusion.refs_0_
  112.4 0.3 collective-permute-done.7.refs_6_
  112.7 0.0 copy-done.5
  112.7 10.0 %shard_map.94.refs_1_ = f32[64,8,2048]{2,1,0:T(8,128)} custom-call(s32[2]{0:T(128)S(1)} %pad_add_fusion.refs_0_, bf16[64,8,2048]{2,1,0:T(8,128)(2,1)S(1)} %copy-done.5, f32[4,1,2048]{2,1,0:T(1,128)S(1)} %broadcast_in_dim_reshape.6.refs_2_, f32[16,1,2048]{2,1,0:T(1,128)S(1)} %tile.11.refs_3_, f32[8,1]{1,0:T(8,128)S(1)} %copy.14.refs_4_, ...), custom_call_target="tpu_custom_call" | custom-call | flops 4294967296 | bytes 8388608 | tf_op jit(solution)/shard_map/pallas_call | solution.py:190
  122.7 0.0 copy-done.3
  122.7 0.0 copy-done.2
  122.7 0.0 copy-done.1
  122.7 8.9 %all-to-all-done.3.refs_6_ = bf16[16,2,8,2048]{3,2,1,0:T(8,128)(2,1)} async-done(((bf16[16,2,8,2048]{3,2,1,0:T(8,128)(2,1)}), bf16[16,2,8,2048]{3,2,1,0:T(8,128)(2,1)}, u32[]{:S(2)}, u32[]{:S(2)}) %all-to-all-start.3) | async-done | bytes 1048608 | tf_op jit(solution)/shard_map/all_to_all | solution.py:305
  131.6 6.7 %shard_map.95 = bf16[8,64,2048]{2,1,0:T(8,128)(2,1)} custom-call(s32[64]{0:T(128)} %refs_0_.3, f32[64,8,2048]{2,1,0:T(8,128)} %shard_map.94.refs_1_, f32[4,1,2048]{2,1,0:T(1,128)} %copy-done.2, f32[16,1,2048]{2,1,0:T(1,128)} %copy-done.1, f32[8,1]{1,0:T(8,128)} %copy-done.3, bf16[16,2,8,2048]{3,2,1,0:T(8,128)(2,1)} %all-to-all-done.2.refs_5_, ...), custom_call_target="tpu_custom_call" | custom-call | flops 8388608 | bytes 8388608 | tf_op jit(solution)/shard_map/pallas_call | solution.py:238
  (4 shorter events, 0.1 us)
Async XLA Ops:
  0.0 13.2 %copy-start = (bf16[64,1024]{1,0:T(8,128)(2,1)S(1)}, bf16[64,1024]{1,0:T(8,128)(2,1)}, u32[]{:S(2)}) copy-start(bf16[64,1024]{1,0:T(8,128)(2,1)} %param.17) | copy-start | bytes 393220
  4.7 43.5 %copy-start.4 = (s32[4]{0:T(128)S(1)}, s32[4]{0:T(128)}, u32[]{:S(2)}) copy-start(s32[4]{0:T(128)} %refs_1_.5) | copy-start | bytes 52
  4.7 34.3 %all-to-all-start = ((bf16[16,2,8,2048]{3,2,1,0:T(8,128)(2,1)}), bf16[16,2,8,2048]{3,2,1,0:T(8,128)(2,1)S(1)}, u32[]{:S(2)}, u32[]{:S(2)}) async-start(bf16[16,2,8,2048]{3,2,1,0:T(8,128)(2,1)} %get-tuple-element.37), calls=%async_computation | async-start | bytes 2097152 | tf_op jit(solution)/shard_map/all_to_all | solution.py:305
  13.2 28.4 %collective-permute-start = (bf16[1,32,1024]{2,1,0:T(8,128)(2,1)S(1)}, bf16[1,32,1024]{2,1,0:T(8,128)(2,1)S(1)}, u32[]{:S(2)}, u32[]{:S(2)}) collective-permute-start(bf16[1,32,1024]{2,1,0:T(8,128)(2,1)S(1)} %dynamic-slice_bitcast_fusion), channel_id=1, source_target_pairs={{0,16},{2,18},{4,20},{6,22},{8,24},{10,26},{12,28},{14,30},{16,0},... | collective-permute-start | bytes 196616 | tf_op jit(solution)/shard_map/ppermute | solution.py:279
  41.6 28.7 %all-to-all-start.1 = ((bf16[16,2,8,2048]{3,2,1,0:T(8,128)(2,1)}), bf16[16,2,8,2048]{3,2,1,0:T(8,128)(2,1)S(1)}, u32[]{:S(2)}, u32[]{:S(2)}) async-start(bf16[16,2,8,2048]{3,2,1,0:T(8,128)(2,1)} %get-tuple-element.39), calls=%async_computation.1 | async-start | bytes 2097152 | tf_op jit(solution)/shard_map/all_to_all | solution.py:305
  46.3 19.1 %collective-permute-start.1 = (bf16[2,32,1024]{2,1,0:T(8,128)(2,1)S(1)}, bf16[2,32,1024]{2,1,0:T(8,128)(2,1)S(1)}, u32[]{:S(2)}, u32[]{:S(2)}) collective-permute-start(bf16[2,32,1024]{2,1,0:T(8,128)(2,1)S(1)} %maximum_bitcast_fusion), channel_id=1, source_target_pairs={{0,8},{2,10},{4,12},{6,14},{8,0},{10,2},{12,4},{14,6},{16,24},{18,... | collective-permute-start | bytes 393224 | tf_op jit(solution)/shard_map/ppermute | solution.py:279
  65.4 3.6 %collective-permute-start.2 = (bf16[16,2,8,2048]{3,2,1,0:T(8,128)(2,1)S(1)}, bf16[16,2,8,2048]{3,2,1,0:T(8,128)(2,1)S(1)}, u32[]{:S(2)}, u32[]{:S(2)}) collective-permute-start(bf16[16,2,8,2048]{3,2,1,0:T(8,128)(2,1)S(1)} %get-tuple-element.47), channel_id=1, source_target_pairs={{0,1},{1,0},{2,3},{3,2},{4,5},{5,4},{6,7},{7,6},{8,9},{9,8},{10,11... | collective-permute-start | bytes 3145736 | tf_op jit(solution)/shard_map/ppermute | solution.py:330
  65.4 29.5 %collective-permute-start.5 = (bf16[4,32,1024]{2,1,0:T(8,128)(2,1)S(1)}, bf16[4,32,1024]{2,1,0:T(8,128)(2,1)S(1)}, u32[]{:S(2)}, u32[]{:S(2)}) collective-permute-start(bf16[4,32,1024]{2,1,0:T(8,128)(2,1)S(1)} %bitcast.27), channel_id=1, source_target_pairs={{0,6},{2,4},{4,2},{6,0},{8,14},{10,12},{12,10},{14,8},{16,22},{18,... | collective-permute-start | bytes 786440 | tf_op jit(solution)/shard_map/ppermute | solution.py:279
  68.2 26.8 %collective-permute-start.4 = (bf16[4,32,1024]{2,1,0:T(8,128)(2,1)S(1)}, bf16[4,32,1024]{2,1,0:T(8,128)(2,1)S(1)}, u32[]{:S(2)}, u32[]{:S(2)}) collective-permute-start(bf16[4,32,1024]{2,1,0:T(8,128)(2,1)S(1)} %bitcast.28), channel_id=1, source_target_pairs={{0,4},{2,6},{4,0},{6,2},{8,12},{10,14},{12,8},{14,10},{16,20},{18,... | collective-permute-start | bytes 786440 | tf_op jit(solution)/shard_map/ppermute | solution.py:279
  68.7 26.3 %collective-permute-start.3 = (bf16[4,32,1024]{2,1,0:T(8,128)(2,1)S(1)}, bf16[4,32,1024]{2,1,0:T(8,128)(2,1)S(1)}, u32[]{:S(2)}, u32[]{:S(2)}) collective-permute-start(bf16[4,32,1024]{2,1,0:T(8,128)(2,1)S(1)} %bitcast.29), channel_id=1, source_target_pairs={{0,2},{2,0},{4,6},{6,4},{8,10},{10,8},{12,14},{14,12},{16,18},{18,... | collective-permute-start | bytes 786440 | tf_op jit(solution)/shard_map/ppermute | solution.py:279
  70.4 32.2 %all-to-all-start.2 = ((bf16[16,2,8,2048]{3,2,1,0:T(8,128)(2,1)}), bf16[16,2,8,2048]{3,2,1,0:T(8,128)(2,1)}, u32[]{:S(2)}, u32[]{:S(2)}) async-start(bf16[16,2,8,2048]{3,2,1,0:T(8,128)(2,1)} %add_convert_fusion.1), calls=%async_computation.2 | async-start | bytes 2097152 | tf_op jit(solution)/shard_map/all_to_all | solution.py:305
  94.9 7.7 %copy-start.6 = (bf16[4,32,1024]{2,1,0:T(8,128)(2,1)}, bf16[4,32,1024]{2,1,0:T(8,128)(2,1)S(1)}, u32[]{:S(2)}) copy-start(bf16[4,32,1024]{2,1,0:T(8,128)(2,1)S(1)} %collective-permute-done.5) | copy-start | bytes 786436
  94.9 7.6 %copy-start.7 = (bf16[4,32,1024]{2,1,0:T(8,128)(2,1)}, bf16[4,32,1024]{2,1,0:T(8,128)(2,1)S(1)}, u32[]{:S(2)}) copy-start(bf16[4,32,1024]{2,1,0:T(8,128)(2,1)S(1)} %collective-permute-done.4) | copy-start | bytes 786436
  94.9 7.6 %copy-start.8 = (bf16[4,32,1024]{2,1,0:T(8,128)(2,1)}, bf16[4,32,1024]{2,1,0:T(8,128)(2,1)S(1)}, u32[]{:S(2)}) copy-start(bf16[4,32,1024]{2,1,0:T(8,128)(2,1)S(1)} %collective-permute-done.3) | copy-start | bytes 786436
  95.0 2.7 %collective-permute-start.6 = (bf16[16,2,8,2048]{3,2,1,0:T(8,128)(2,1)S(1)}, bf16[16,2,8,2048]{3,2,1,0:T(8,128)(2,1)S(1)}, u32[]{:S(2)}, u32[]{:S(2)}) collective-permute-start(bf16[16,2,8,2048]{3,2,1,0:T(8,128)(2,1)S(1)} %get-tuple-element.55), channel_id=1, source_target_pairs={{0,1},{1,0},{2,3},{3,2},{4,5},{5,4},{6,7},{7,6},{8,9},{9,8},{10,11... | collective-permute-start | bytes 3145736 | tf_op jit(solution)/shard_map/ppermute | solution.py:330
  99.0 10.9 %copy-start.9 = (f32[1024]{0:T(1024)S(1)}, f32[1024]{0:T(1024)}, u32[]{:S(2)}) copy-start(f32[1024]{0:T(1024)} %param.15) | copy-start | bytes 12292
  99.0 10.9 %slice-start = ((f32[1024]{0:T(1024)}), f32[256]{0:T(256)S(1)}, s32[]{:S(2)}) async-start(f32[1024]{0:T(1024)} %param.15), calls=%async_computation.4 | async-start | bytes 2048 | tf_op jit(solution)/shard_map/slice | solution.py:349
  99.0 11.0 %copy-start.10 = (f32[8]{0:T(128)S(1)}, f32[8]{0:T(128)}, u32[]{:S(2)}) copy-start(f32[8]{0:T(128)} %param.16) | copy-start | bytes 100
  99.0 13.6 %copy-start.5 = (bf16[64,8,2048]{2,1,0:T(8,128)(2,1)S(1)}, bf16[64,8,2048]{2,1,0:T(8,128)(2,1)}, u32[]{:S(2)}) copy-start(bf16[64,8,2048]{2,1,0:T(8,128)(2,1)} %get-tuple-element.36.refs_1_) | copy-start | bytes 6291460
  102.6 29.0 %all-to-all-start.3 = ((bf16[16,2,8,2048]{3,2,1,0:T(8,128)(2,1)}), bf16[16,2,8,2048]{3,2,1,0:T(8,128)(2,1)}, u32[]{:S(2)}, u32[]{:S(2)}) async-start(bf16[16,2,8,2048]{3,2,1,0:T(8,128)(2,1)} %add_convert_fusion), calls=%async_computation.3 | async-start | bytes 2097152 | tf_op jit(solution)/shard_map/all_to_all | solution.py:305
  109.8 2.9 %collective-permute-start.7 = (bf16[1,16,32,1024]{3,2,1,0:T(8,128)(2,1)S(1)}, bf16[1,16,32,1024]{3,2,1,0:T(8,128)(2,1)}, u32[]{:S(2)}, u32[]{:S(2)}) collective-permute-start(bf16[1,16,32,1024]{3,2,1,0:T(8,128)(2,1)S(1)} %bitcast.25), channel_id=1, source_target_pairs={{0,1},{1,0},{2,3},{3,2},{4,5},{5,4},{6,7},{7,6},{8,9},{9,8},{10,11... | collective-permute-start | bytes 3145736 | tf_op jit(solution)/shard_map/ppermute | solution.py:279
  110.2 12.6 %copy-start.3 = (f32[8,1]{1,0:T(8,128)}, f32[8,1]{1,0:T(8,128)S(1)}, u32[]{:S(2)}) copy-start(f32[8,1]{1,0:T(8,128)S(1)} %copy.14.refs_4_) | copy-start | bytes 100
  110.4 12.3 %copy-start.2 = (f32[4,1,2048]{2,1,0:T(1,128)}, f32[4,1,2048]{2,1,0:T(1,128)S(1)}, u32[]{:S(2)}) copy-start(f32[4,1,2048]{2,1,0:T(1,128)S(1)} %broadcast_in_dim_reshape.6.refs_2_) | copy-start | bytes 98308
  112.3 10.4 %copy-start.1 = (f32[16,1,2048]{2,1,0:T(1,128)}, f32[16,1,2048]{2,1,0:T(1,128)S(1)}, u32[]{:S(2)}) copy-start(f32[16,1,2048]{2,1,0:T(1,128)S(1)} %tile.11.refs_3_) | copy-start | bytes 393220

commit v2 on v1

--- a/solution.py
+++ b/solution.py
@@ -12,28 +12,38 @@
 MIB = 1 << 20
 
 
-def prepare_kernel(owners, in_tiles_ref, amps_ref, mask_ref, tiles_ref, *sent_refs):
-    tile_count = amps_ref.shape[1]
-    swapped = jnp.swapaxes(amps_ref[...].astype(jnp.float32), 0, 1)
-    for tile in range(tile_count):
-        kept = jnp.where(mask_ref[:, tile : tile + 1] > 0, swapped[tile], 0.0)
-        tiles_ref[tile] = kept.astype(tiles_ref.dtype)
-    size = tile_count // owners // len(sent_refs)
-    for chunk, sent_ref in enumerate(sent_refs):
+def selection(tile, tile_count, pairs):
+    shape = (pairs, pairs * tile_count)
+    column = lax.broadcasted_iota(jnp.int32, shape, 1)
+    return column == lax.broadcasted_iota(jnp.int32, shape, 0) * tile_count + tile
+
+
+def first_kernel(chunks, in_tiles_ref, amps_ref, mask_ref, sent_ref, picks):
+    pairs, tile_count, width = amps_ref.shape
+    owners, size = sent_ref.shape[:2]
+
+    @pl.when(pl.program_id(0) == 0)
+    def _():
+        mask = jnp.concatenate([mask_ref[...]] * pairs, axis=1) > 0
         for owner in range(owners):
             for slot in range(size):
-                source = in_tiles_ref[(owner * len(sent_refs) + chunk) * size + slot]
-                sent_ref[owner, slot] = tiles_ref[source]
-
-
-def prepare(in_tiles, amps, amp_mask, owners, chunks):
+                tile = in_tiles_ref[owner * chunks * size + slot]
+                row = (owner * size + slot) * pairs
+                picked = selection(tile, tile_count, pairs) & mask
+                picks[row : row + pairs] = jnp.where(picked, 1.0, 0.0)
+
+    amps = amps_ref[...].reshape(pairs * tile_count, width)
+    rows = jnp.dot(picks[...].astype(amps.dtype), amps, preferred_element_type=jnp.float32)
+    sent_ref[...] = rows.reshape(sent_ref.shape).astype(sent_ref.dtype)
+
+
+def prepare_first(in_tiles, amps, amp_mask, owners, chunks):
     pairs, tiles, share = amps.shape
     width = min(share, 1024)
     size = tiles // owners // chunks
     return pl.pallas_call(
-        lambda *refs: prepare_kernel(owners, *refs),
-        out_shape=(jax.ShapeDtypeStruct((tiles, pairs, share), amps.dtype),)
-        + (jax.ShapeDtypeStruct((owners, size, pairs, share), amps.dtype),) * chunks,
+        lambda *refs: first_kernel(chunks, *refs),
+        out_shape=jax.ShapeDtypeStruct((owners, size, pairs, share), amps.dtype),
         grid_spec=pltpu.PrefetchScalarGridSpec(
             num_scalar_prefetch=1,
             grid=(share // width,),
@@ -41,8 +51,50 @@
                 pl.BlockSpec((pairs, tiles, width), lambda i, _: (0, 0, i)),
                 pl.BlockSpec((pairs, tiles), lambda i, _: (0, 0)),
             ],
+            out_specs=pl.BlockSpec((owners, size, pairs, width), lambda i, _: (0, 0, 0, i)),
+            scratch_shapes=[pltpu.VMEM((owners * size * pairs, pairs * tiles), jnp.float32)],
+        ),
+        compiler_params=pltpu.CompilerParams(vmem_limit_bytes=56 * MIB),
+        cost_estimate=pl.CostEstimate(
+            flops=2 * pairs * pairs * tiles * tiles * share // chunks,
+            bytes_accessed=3 * pairs * tiles * share,
+            transcendentals=0,
+        ),
+    )(in_tiles, amps, amp_mask)
+
+
+def prepare_kernel(owners, chunks, in_tiles_ref, amps_ref, mask_ref, tiles_ref, *sent_refs):
+    tile_count = amps_ref.shape[1]
+    swapped = jnp.swapaxes(amps_ref[...].astype(jnp.float32), 0, 1)
+    for tile in range(tile_count):
+        kept = jnp.where(mask_ref[:, tile : tile + 1] > 0, swapped[tile], 0.0)
+        tiles_ref[tile] = kept.astype(tiles_ref.dtype)
+    size = tile_count // owners // chunks
+    for chunk, sent_ref in enumerate(sent_refs, start=1):
+        for owner in range(owners):
+            for slot in range(size):
+                source = in_tiles_ref[(owner * chunks + chunk) * size + slot]
+                sent_ref[owner, slot] = tiles_ref[source]
+
+
+def prepare(in_tiles, amps, amp_mask, owners, chunks):
+    pairs, tiles, share = amps.shape
+    width = min(share, 1024)
+    size = tiles // owners // chunks
+    return pl.pallas_call(
+        lambda *refs: prepare_kernel(owners, chunks, *refs),
+        out_shape=(jax.ShapeDtypeStruct((tiles, pairs, share), amps.dtype),)
+        + (jax.ShapeDtypeStruct((owners, size, pairs, share), amps.dtype),) * (chunks - 1),
+        grid_spec=pltpu.PrefetchScalarGridSpec(
+            num_scalar_prefetch=1,
+            grid=(share // width,),
+            in_specs=[
+                pl.BlockSpec((pairs, tiles, width), lambda i, _: (0, 0, i)),
+                pl.BlockSpec((pairs, tiles), lambda i, _: (0, 0)),
+            ],
             out_specs=[pl.BlockSpec((tiles, pairs, width), lambda i, _: (0, 0, i))]
-            + [pl.BlockSpec((owners, size, pairs, width), lambda i, _: (0, 0, 0, i))] * chunks,
+            + [pl.BlockSpec((owners, size, pairs, width), lambda i, _: (0, 0, 0, i))]
+            * (chunks - 1),
         ),
         compiler_params=pltpu.CompilerParams(vmem_limit_bytes=56 * MIB),
         cost_estimate=pl.CostEstimate(
@@ -54,20 +106,25 @@
 
 
 def ladder_kernel(first_slot, index_ref, keep_ref, x_ref, w_ref, *rest):
-    out_refs, x_rows = rest[:-1], rest[-1]
+    out_refs, (x_columns, sums) = rest[:-2], rest[-2:]
     part, slot, block = pl.program_id(0), pl.program_id(1), pl.program_id(2)
-    rows, depth = x_rows.shape
-
-    @pl.when(block == 0)
+    depth, rows = x_columns.shape[1:]
+    step = min(depth, 256)
+
+    @pl.when((part == 0) & (block == 0))
     def _():
         x = x_ref[:, 0].astype(jnp.float32).reshape(rows, depth)
-        x_rows[...] = x.astype(x_rows.dtype)
-
+        x_columns[slot] = x.T.astype(x_columns.dtype)
+
+    for k in range(0, depth, step):
+        product = jnp.dot(
+            w_ref[0, :, k : k + step],
+            x_columns[slot, k : k + step],
+            preferred_element_type=jnp.float32,
+        )
+        sums[...] = product if k == 0 else sums[...] + product
     keep = keep_ref[first_slot + slot] > 0
-    product = lax.dot_general(
-        x_rows[...], w_ref[0], (((1,), (1,)), ((), ())), preferred_element_type=jnp.float32
-    )
-    product = jnp.where(keep, product, 0.0)
+    product = jnp.where(keep, sums[...].T, 0.0)
     for index, out_ref in enumerate(out_refs):
 
         @pl.when(part == index)
@@ -114,9 +171,12 @@
             out_specs=[
                 pl.BlockSpec((owners, 1, pairs, width), out_map(index)) for index in range(parts)
             ],
-            scratch_shapes=[pltpu.VMEM((owners * pairs, depth), received.dtype)],
-        ),
-        compiler_params=pltpu.CompilerParams(vmem_limit_bytes=24 * MIB),
+            scratch_shapes=[
+                pltpu.VMEM((chunk_slots, depth, owners * pairs), received.dtype),
+                pltpu.VMEM((width, owners * pairs), jnp.float32),
+            ],
+        ),
+        compiler_params=pltpu.CompilerParams(vmem_limit_bytes=32 * MIB),
         cost_estimate=pl.CostEstimate(
             flops=2 * owners * pairs * chunk_slots * entries * depth,
             bytes_accessed=2 * chunk_slots * entries * depth,
@@ -234,7 +294,7 @@
 
 def finish(out_tiles, base, first, second, pair_energy, parts, dtype):
     count, pairs, share = base.shape
-    width = min(share, 512)
+    width = min(share, 1024)
     return pl.pallas_call(
         lambda *refs: finish_kernel(len(parts), *refs),
         out_shape=jax.ShapeDtypeStruct((pairs, count, share), dtype),
@@ -299,7 +359,9 @@
         strip = share // TILE
         int_index = lax.axis_index("int")
 
-        masked, *sent = prepare(in_tiles, amps, amp_mask, owners, chunks)
+        sent = [prepare_first(in_tiles, amps, amp_mask, owners, chunks)]
+        masked, *later = prepare(in_tiles, amps, amp_mask, owners, chunks)
+        sent += later
 
         def exchanged(part):
             return lax.all_to_all(part, "pair", split_axis=0, concat_axis=0, tiled=True)
@@ -310,6 +372,9 @@
         gathered = [lax.dynamic_slice_in_dim(dressing, int_index * own, own, 0)[None]]
         together = lax.optimization_barrier
         received, returned = [], []
+        if steps:
+            gathered = exchange(joined(gathered), steps.pop(0))
+            sent[0], gathered = together((sent[0], gathered))
         for c in range(chunks):
             if c:
                 received[-1], sent[c] = together((received[-1], sent[c]))
@@ -319,12 +384,14 @@
                 gathered = exchange(joined(gathered), steps.pop(0))
             if c == 0:
                 received[c], gathered = together((received[c], gathered))
-            if steps:
+            if c == 0 and steps:
                 gathered = exchange(joined(gathered), steps.pop(0))
             terms = ladder(
                 int_index.astype(jnp.int32)[None], block_mask, received[c], integrals, c, parts
             )
-            (*others, total), gathered = together((terms, gathered))
+            if c:
+                terms, gathered = together((terms, gathered))
+            *others, total = terms
             total = total.astype(jnp.float32)
             for r, other in enumerate(others):
                 got = lax.ppermute(

time: 139 us -> 133 us (0.957)
  waiting for transfers between devices: 41.5 us -> 35 us
    pallas_call x1 -> x2, Pallas kernels: 4.7 us -> 8.11 us  [the longest x1 4.35 us: prepare(): pl.pallas_call(lambda *refs: prepare_kernel(owners, chunks, *refs), out_s...]
    all_to_all x4, waiting for transfers between devices: 35.3 us -> 32 us  [exchanged(): return lax.all_to_all(part, 'pair', split_axis=0, concat_axis=0, tiled=True)]
    ppermute x6, waiting for transfers between devices: 3.55 us -> 0.33 us  [exchange(): lax.ppermute(block, axis, [(j, j ^ distance) for j in range(size)])]
    all_to_all x4, starting transfers between devices: 27 us -> 24.8 us  [exchanged(): return lax.all_to_all(part, 'pair', split_axis=0, concat_axis=0, tiled=True)]
    pallas_call x2, Pallas kernels: 33.1 us -> 31.4 us  [ladder(): pl.pallas_call(lambda *refs: ladder_kernel(first_slot, *refs), out_shape=...]
  transfers between devices with their start and end apart: 12 -> 12, of which waited for: 7 -> 6; matrix products, arithmetic and copies ran while one was open for 5% -> 5% of each run, Pallas kernels for 31% -> 37%
where the time goes in v2:
time: 133 us
  Pallas kernels  55.3 us (42%)
  waiting for transfers between devices  35 us (26%)
  starting transfers between devices  34.6 us (26%)
  other arithmetic  4.14 us (3%)
  local copies, waits for them, and re-layouts  3.29 us (2%)
    all_to_all x4, waiting for transfers between devices, exchanged(): return lax.all_to_all(part, 'pair', split_axis=0, concat_axis=0, tiled=True)  32 us
    pallas_call x2, Pallas kernels, ladder(): pl.pallas_call(lambda *refs: ladder_kernel(first_slot, *refs), out_shape=...  31.4 us
    all_to_all x4, starting transfers between devices, exchanged(): return lax.all_to_all(part, 'pair', split_axis=0, concat_axis=0, tiled=True)  24.8 us
    pallas_call x1, Pallas kernels, cycle_terms(): pl.pallas_call(lambda *refs: cycle_kernel(owners, parts, *refs), out_shap...  10 us
    ppermute x6, starting transfers between devices, exchange(): lax.ppermute(block, axis, [(j, j ^ distance) for j in range(size)])  9.65 us
    pallas_call x1, Pallas kernels, finish(): pl.pallas_call(lambda *refs: finish_kernel(len(parts), *refs), out_shape=...  5.73 us
    pallas_call x1, Pallas kernels, prepare(): pl.pallas_call(lambda *refs: prepare_kernel(owners, chunks, *refs), out_s...  4.35 us
    pallas_call x1, Pallas kernels, prepare_first(): pl.pallas_call(lambda *refs: first_kernel(chunks, *refs), out_shape=jax.S...  3.76 us
  transfers between devices with their start and end apart: 12, of which 6 were waited for; matrix products, arithmetic and copies ran while one was open for 5% of the time, Pallas kernels for 37%

profile of v2, /device:TPU:0, one launch (start us, length us, event | category | flops | bytes accessed | tf_op | source)
XLA Modules:
  0.0 132.5 jit_solution(11258922881367195594)
XLA Ops:
  0.0 0.0 copy-start
  0.0 0.9 copy-done
  0.9 4.0 %collective-permute-start = (bf16[1,32,1024]{2,1,0:T(8,128)(2,1)S(1)}, bf16[1,32,1024]{2,1,0:T(8,128)(2,1)S(1)}, u32[]{:S(2)}, u32[]{:S(2)}) collective-permute-start(bf16[1,32,1024]{2,1,0:T(8,128)(2,1)S(1)} %dynamic-slice_bitcast_fusion), channel_id=1, source_target_pairs={{0,16},{2,18},{4,20},{6,22},{8,24},{10,26},{12,28},{14,30},{16,0},... | collective-permute-start | bytes 196616 | tf_op jit(solution)/shard_map/ppermute | solution.py:339
  4.9 3.8 %shard_map.92 = bf16[16,2,8,2048]{3,2,1,0:T(8,128)(2,1)} custom-call(s32[64]{0:T(128)} %refs_0_.4, bf16[8,64,2048]{2,1,0:T(8,128)(2,1)} %refs_1_.5, s32[8,64]{1,0:T(8,128)} %refs_2_.3), custom_call_target="tpu_custom_call" | custom-call | flops 536870912 | bytes 3145728 | tf_op jit(solution)/shard_map/pallas_call | solution.py:44
  8.7 0.0 collective-permute-done
  8.7 6.5 %all-to-all-start = ((bf16[16,2,8,2048]{3,2,1,0:T(8,128)(2,1)}), bf16[16,2,8,2048]{3,2,1,0:T(8,128)(2,1)S(1)}, u32[]{:S(2)}, u32[]{:S(2)}) async-start(bf16[16,2,8,2048]{3,2,1,0:T(8,128)(2,1)} %shard_map.92), calls=%async_computation | async-start | bytes 2097152 | tf_op jit(solution)/shard_map/all_to_all | solution.py:367
  15.3 0.0 copy-start.4
  15.3 2.0 %collective-permute-start.1 = (bf16[2,32,1024]{2,1,0:T(8,128)(2,1)S(1)}, bf16[2,32,1024]{2,1,0:T(8,128)(2,1)S(1)}, u32[]{:S(2)}, u32[]{:S(2)}) collective-permute-start(bf16[2,32,1024]{2,1,0:T(8,128)(2,1)S(1)} %maximum_bitcast_fusion), channel_id=1, source_target_pairs={{0,8},{2,10},{4,12},{6,14},{8,0},{10,2},{12,4},{14,6},{16,24},{18,... | collective-permute-start | bytes 393224 | tf_op jit(solution)/shard_map/ppermute | solution.py:339
  17.3 4.4 %shard_map.91 = (bf16[64,8,2048]{2,1,0:T(8,128)(2,1)}, bf16[16,2,8,2048]{3,2,1,0:T(8,128)(2,1)}) custom-call(s32[64]{0:T(128)} %refs_0_.4, bf16[8,64,2048]{2,1,0:T(8,128)(2,1)} %refs_1_.5, s32[8,64]{1,0:T(8,128)} %refs_2_.3), custom_call_target="tpu_custom_call" | custom-call | flops 2097152 | bytes 6291456 | tf_op jit(solution)/shard_map/pallas_call | solution.py:84
  21.6 17.9 %all-to-all-done.refs_2_ = bf16[16,2,8,2048]{3,2,1,0:T(8,128)(2,1)S(1)} async-done(((bf16[16,2,8,2048]{3,2,1,0:T(8,128)(2,1)}), bf16[16,2,8,2048]{3,2,1,0:T(8,128)(2,1)S(1)}, u32[]{:S(2)}, u32[]{:S(2)}) %all-to-all-start) | async-done | bytes 1048608 | tf_op jit(solution)/shard_map/all_to_all | solution.py:367
  39.5 0.0 collective-permute-done.1
  39.5 5.8 %all-to-all-start.1 = ((bf16[16,2,8,2048]{3,2,1,0:T(8,128)(2,1)}), bf16[16,2,8,2048]{3,2,1,0:T(8,128)(2,1)S(1)}, u32[]{:S(2)}, u32[]{:S(2)}) async-start(bf16[16,2,8,2048]{3,2,1,0:T(8,128)(2,1)} %get-tuple-element.37), calls=%async_computation.1 | async-start | bytes 2097152 | tf_op jit(solution)/shard_map/all_to_all | solution.py:367
  45.4 0.0 copy-done.4
  45.4 15.7 %shard_map.93 = (bf16[16,2,8,2048]{3,2,1,0:T(8,128)(2,1)S(1)}, bf16[16,2,8,2048]{3,2,1,0:T(8,128)(2,1)S(1)}) custom-call(s32[1]{0:T(128)} %bitcast.1.refs_0_, s32[4]{0:T(128)S(1)} %copy-done.4, bf16[16,2,8,2048]{3,2,1,0:T(8,128)(2,1)S(1)} %all-to-all-done.refs_2_, bf16[4,4096,2048]{2,1,0:T(8,128)(2,1)} %refs_3_.3), custom_call_target="tpu_custom_call" | custom-call | flops 4294967296 | bytes 33554432 | tf_op jit(solution)/shard_map/pallas_call | solution.py:156
  61.1 0.1 collective-permute-start.2
  61.2 2.9 %collective-permute-start.5 = (bf16[4,32,1024]{2,1,0:T(8,128)(2,1)S(1)}, bf16[4,32,1024]{2,1,0:T(8,128)(2,1)S(1)}, u32[]{:S(2)}, u32[]{:S(2)}) collective-permute-start(bf16[4,32,1024]{2,1,0:T(8,128)(2,1)S(1)} %bitcast.27), channel_id=1, source_target_pairs={{0,6},{2,4},{4,2},{6,0},{8,14},{10,12},{12,10},{14,8},{16,22},{18,... | collective-permute-start | bytes 786440 | tf_op jit(solution)/shard_map/ppermute | solution.py:339
  64.1 0.6 collective-permute-start.4
  64.6 0.1 collective-permute-start.3
  64.7 0.0 collective-permute-done.2
  64.8 1.4 %add_convert_fusion.1 = bf16[16,2,8,2048]{3,2,1,0:T(8,128)(2,1)} fusion(bf16[16,2,8,2048]{3,2,1,0:T(8,128)(2,1)S(1)} %collective-permute-done.2, bf16[16,2,8,2048]{3,2,1,0:T(8,128)(2,1)S(1)} %get-tuple-element.42), kind=kLoop, calls=%fused_computation.1 | loop fusion | flops 2097152 | bytes 3145728 | tf_op jit(solution)/shard_map/convert_element_type | solution.py:401
  66.1 2.3 %all-to-all-done.1.refs_2_ = bf16[16,2,8,2048]{3,2,1,0:T(8,128)(2,1)S(1)} async-done(((bf16[16,2,8,2048]{3,2,1,0:T(8,128)(2,1)}), bf16[16,2,8,2048]{3,2,1,0:T(8,128)(2,1)S(1)}, u32[]{:S(2)}, u32[]{:S(2)}) %all-to-all-start.1) | async-done | bytes 1048608 | tf_op jit(solution)/shard_map/all_to_all | solution.py:367
  68.4 6.3 %all-to-all-start.2 = ((bf16[16,2,8,2048]{3,2,1,0:T(8,128)(2,1)}), bf16[16,2,8,2048]{3,2,1,0:T(8,128)(2,1)S(1)}, u32[]{:S(2)}, u32[]{:S(2)}) async-start(bf16[16,2,8,2048]{3,2,1,0:T(8,128)(2,1)} %add_convert_fusion.1), calls=%async_computation.2 | async-start | bytes 2097152 | tf_op jit(solution)/shard_map/all_to_all | solution.py:367
  74.7 15.7 %shard_map.94 = (bf16[16,2,8,2048]{3,2,1,0:T(8,128)(2,1)S(1)}, bf16[16,2,8,2048]{3,2,1,0:T(8,128)(2,1)S(1)}) custom-call(s32[1]{0:T(128)} %bitcast.1.refs_0_, s32[4]{0:T(128)S(1)} %copy-done.4, bf16[16,2,8,2048]{3,2,1,0:T(8,128)(2,1)S(1)} %all-to-all-done.1.refs_2_, bf16[4,4096,2048]{2,1,0:T(8,128)(2,1)} %refs_3_.3), custom_call_target="tpu_custom_call" | custom-call | flops 4294967296 | bytes 33554432 | tf_op jit(solution)/shard_map/pallas_call | solution.py:156
  90.4 0.0 collective-permute-done.5
  90.4 0.0 copy-start.7
  90.4 0.0 collective-permute-done.4
  90.4 0.0 copy-start.8
  90.4 0.0 collective-permute-done.3
  90.4 0.0 copy-start.9
  90.4 0.1 collective-permute-start.6
  90.5 2.6 %collective-permute-done.6 = bf16[16,2,8,2048]{3,2,1,0:T(8,128)(2,1)S(1)} collective-permute-done((bf16[16,2,8,2048]{3,2,1,0:T(8,128)(2,1)S(1)}, bf16[16,2,8,2048]{3,2,1,0:T(8,128)(2,1)S(1)}, u32[]{:S(2)}, u32[]{:S(2)}) %collective-permute-start.6) | collective-permute-done | bytes 1048608 | tf_op jit(solution)/shard_map/ppermute | solution.py:397
  93.2 0.0 copy-done.7
  93.2 0.0 copy-done.8
  93.2 0.0 copy-done.9
  93.2 1.4 %add_convert_fusion = bf16[16,2,8,2048]{3,2,1,0:T(8,128)(2,1)} fusion(bf16[16,2,8,2048]{3,2,1,0:T(8,128)(2,1)S(1)} %collective-permute-done.6, bf16[16,2,8,2048]{3,2,1,0:T(8,128)(2,1)S(1)} %get-tuple-element.50), kind=kLoop, calls=%fused_computation | loop fusion | flops 2097152 | bytes 3145728 | tf_op jit(solution)/shard_map/convert_element_type | solution.py:401
  94.6 0.0 copy-start.10
  94.6 0.0 slice-start
  94.6 3.1 %all-to-all-done.2.refs_5_ = bf16[16,2,8,2048]{3,2,1,0:T(8,128)(2,1)S(1)} async-done(((bf16[16,2,8,2048]{3,2,1,0:T(8,128)(2,1)}), bf16[16,2,8,2048]{3,2,1,0:T(8,128)(2,1)S(1)}, u32[]{:S(2)}, u32[]{:S(2)}) %all-to-all-start.2) | async-done | bytes 1048608 | tf_op jit(solution)/shard_map/all_to_all | solution.py:367
  97.7 6.1 %all-to-all-start.3 = ((bf16[16,2,8,2048]{3,2,1,0:T(8,128)(2,1)}), bf16[16,2,8,2048]{3,2,1,0:T(8,128)(2,1)}, u32[]{:S(2)}, u32[]{:S(2)}) async-start(bf16[16,2,8,2048]{3,2,1,0:T(8,128)(2,1)} %add_convert_fusion), calls=%async_computation.3 | async-start | bytes 2097152 | tf_op jit(solution)/shard_map/all_to_all | solution.py:367
  103.8 0.0 copy-done.6
  103.8 1.2 pad_maximum_fusion
  105.1 0.1 collective-permute-start.7
  105.2 0.0 copy-done.10
  105.2 0.1 tile.9
  105.2 0.0 slice-done
  105.2 0.1 slice.15
  105.3 0.0 copy-done.11
  105.3 0.1 copy.14.refs_4_
  105.4 0.1 constant_dynamic-slice_fusion
  105.5 0.1 broadcast_in_dim.11
  105.6 0.1 broadcast_in_dim_reshape.6.refs_2_
  105.7 0.0 copy-start.2
  105.7 0.7 tile.10
  106.4 1.1 tile.11.refs_3_
  107.5 0.0 copy-start.1
  107.5 0.1 pad_add_fusion.refs_0_
  107.6 0.3 collective-permute-done.7.refs_6_
  107.9 0.0 copy-done.5
  107.9 10.0 %shard_map.95.refs_1_ = f32[64,8,2048]{2,1,0:T(8,128)} custom-call(s32[2]{0:T(128)S(1)} %pad_add_fusion.refs_0_, bf16[64,8,2048]{2,1,0:T(8,128)(2,1)S(1)} %copy-done.5, f32[4,1,2048]{2,1,0:T(1,128)S(1)} %broadcast_in_dim_reshape.6.refs_2_, f32[16,1,2048]{2,1,0:T(1,128)S(1)} %tile.11.refs_3_, f32[8,1]{1,0:T(8,128)S(1)} %copy.14.refs_4_, ...), custom_call_target="tpu_custom_call" | custom-call | flops 4294967296 | bytes 8388608 | tf_op jit(solution)/shard_map/pallas_call | solution.py:250
  118.0 0.0 copy-done.3
  118.0 0.0 copy-done.2
  118.0 0.0 copy-done.1
  118.0 8.8 %all-to-all-done.3.refs_6_ = bf16[16,2,8,2048]{3,2,1,0:T(8,128)(2,1)} async-done(((bf16[16,2,8,2048]{3,2,1,0:T(8,128)(2,1)}), bf16[16,2,8,2048]{3,2,1,0:T(8,128)(2,1)}, u32[]{:S(2)}, u32[]{:S(2)}) %all-to-all-start.3) | async-done | bytes 1048608 | tf_op jit(solution)/shard_map/all_to_all | solution.py:367
  126.8 5.7 %shard_map.96 = bf16[8,64,2048]{2,1,0:T(8,128)(2,1)} custom-call(s32[64]{0:T(128)} %refs_0_.5, f32[64,8,2048]{2,1,0:T(8,128)} %shard_map.95.refs_1_, f32[4,1,2048]{2,1,0:T(1,128)} %copy-done.2, f32[16,1,2048]{2,1,0:T(1,128)} %copy-done.1, f32[8,1]{1,0:T(8,128)} %copy-done.3, bf16[16,2,8,2048]{3,2,1,0:T(8,128)(2,1)} %copy-done.6, ...), custom_call_target="tpu_custom_call" | custom-call | flops 8388608 | bytes 8388608 | tf_op jit(solution)/shard_map/pallas_call | solution.py:298
  (7 shorter events, 0.1 us)
Async XLA Ops:
  0.0 0.9 copy-start
  0.9 7.8 %collective-permute-start = (bf16[1,32,1024]{2,1,0:T(8,128)(2,1)S(1)}, bf16[1,32,1024]{2,1,0:T(8,128)(2,1)S(1)}, u32[]{:S(2)}, u32[]{:S(2)}) collective-permute-start(bf16[1,32,1024]{2,1,0:T(8,128)(2,1)S(1)} %dynamic-slice_bitcast_fusion), channel_id=1, source_target_pairs={{0,16},{2,18},{4,20},{6,22},{8,24},{10,26},{12,28},{14,30},{16,0},... | collective-permute-start | bytes 196616 | tf_op jit(solution)/shard_map/ppermute | solution.py:339
  8.7 30.8 %all-to-all-start = ((bf16[16,2,8,2048]{3,2,1,0:T(8,128)(2,1)}), bf16[16,2,8,2048]{3,2,1,0:T(8,128)(2,1)S(1)}, u32[]{:S(2)}, u32[]{:S(2)}) async-start(bf16[16,2,8,2048]{3,2,1,0:T(8,128)(2,1)} %shard_map.92), calls=%async_computation | async-start | bytes 2097152 | tf_op jit(solution)/shard_map/all_to_all | solution.py:367
  15.3 30.1 %copy-start.4 = (s32[4]{0:T(128)S(1)}, s32[4]{0:T(128)}, u32[]{:S(2)}) copy-start(s32[4]{0:T(128)} %refs_1_.7) | copy-start | bytes 52
  15.3 24.2 %collective-permute-start.1 = (bf16[2,32,1024]{2,1,0:T(8,128)(2,1)S(1)}, bf16[2,32,1024]{2,1,0:T(8,128)(2,1)S(1)}, u32[]{:S(2)}, u32[]{:S(2)}) collective-permute-start(bf16[2,32,1024]{2,1,0:T(8,128)(2,1)S(1)} %maximum_bitcast_fusion), channel_id=1, source_target_pairs={{0,8},{2,10},{4,12},{6,14},{8,0},{10,2},{12,4},{14,6},{16,24},{18,... | collective-permute-start | bytes 393224 | tf_op jit(solution)/shard_map/ppermute | solution.py:339
  39.5 28.8 %all-to-all-start.1 = ((bf16[16,2,8,2048]{3,2,1,0:T(8,128)(2,1)}), bf16[16,2,8,2048]{3,2,1,0:T(8,128)(2,1)S(1)}, u32[]{:S(2)}, u32[]{:S(2)}) async-start(bf16[16,2,8,2048]{3,2,1,0:T(8,128)(2,1)} %get-tuple-element.37), calls=%async_computation.1 | async-start | bytes 2097152 | tf_op jit(solution)/shard_map/all_to_all | solution.py:367
  61.1 3.7 %collective-permute-start.2 = (bf16[16,2,8,2048]{3,2,1,0:T(8,128)(2,1)S(1)}, bf16[16,2,8,2048]{3,2,1,0:T(8,128)(2,1)S(1)}, u32[]{:S(2)}, u32[]{:S(2)}) collective-permute-start(bf16[16,2,8,2048]{3,2,1,0:T(8,128)(2,1)S(1)} %get-tuple-element.43), channel_id=1, source_target_pairs={{0,1},{1,0},{2,3},{3,2},{4,5},{5,4},{6,7},{7,6},{8,9},{9,8},{10,11... | collective-permute-start | bytes 3145736 | tf_op jit(solution)/shard_map/ppermute | solution.py:397
  61.2 29.2 %collective-permute-start.5 = (bf16[4,32,1024]{2,1,0:T(8,128)(2,1)S(1)}, bf16[4,32,1024]{2,1,0:T(8,128)(2,1)S(1)}, u32[]{:S(2)}, u32[]{:S(2)}) collective-permute-start(bf16[4,32,1024]{2,1,0:T(8,128)(2,1)S(1)} %bitcast.27), channel_id=1, source_target_pairs={{0,6},{2,4},{4,2},{6,0},{8,14},{10,12},{12,10},{14,8},{16,22},{18,... | collective-permute-start | bytes 786440 | tf_op jit(solution)/shard_map/ppermute | solution.py:339
  64.1 26.3 %collective-permute-start.4 = (bf16[4,32,1024]{2,1,0:T(8,128)(2,1)S(1)}, bf16[4,32,1024]{2,1,0:T(8,128)(2,1)S(1)}, u32[]{:S(2)}, u32[]{:S(2)}) collective-permute-start(bf16[4,32,1024]{2,1,0:T(8,128)(2,1)S(1)} %bitcast.28), channel_id=1, source_target_pairs={{0,4},{2,6},{4,0},{6,2},{8,12},{10,14},{12,8},{14,10},{16,20},{18,... | collective-permute-start | bytes 786440 | tf_op jit(solution)/shard_map/ppermute | solution.py:339
  64.6 25.8 %collective-permute-start.3 = (bf16[4,32,1024]{2,1,0:T(8,128)(2,1)S(1)}, bf16[4,32,1024]{2,1,0:T(8,128)(2,1)S(1)}, u32[]{:S(2)}, u32[]{:S(2)}) collective-permute-start(bf16[4,32,1024]{2,1,0:T(8,128)(2,1)S(1)} %bitcast.29), channel_id=1, source_target_pairs={{0,2},{2,0},{4,6},{6,4},{8,10},{10,8},{12,14},{14,12},{16,18},{18,... | collective-permute-start | bytes 786440 | tf_op jit(solution)/shard_map/ppermute | solution.py:339
  68.4 29.3 %all-to-all-start.2 = ((bf16[16,2,8,2048]{3,2,1,0:T(8,128)(2,1)}), bf16[16,2,8,2048]{3,2,1,0:T(8,128)(2,1)S(1)}, u32[]{:S(2)}, u32[]{:S(2)}) async-start(bf16[16,2,8,2048]{3,2,1,0:T(8,128)(2,1)} %add_convert_fusion.1), calls=%async_computation.2 | async-start | bytes 2097152 | tf_op jit(solution)/shard_map/all_to_all | solution.py:367
  90.4 2.8 %copy-start.7 = (bf16[4,32,1024]{2,1,0:T(8,128)(2,1)}, bf16[4,32,1024]{2,1,0:T(8,128)(2,1)S(1)}, u32[]{:S(2)}) copy-start(bf16[4,32,1024]{2,1,0:T(8,128)(2,1)S(1)} %collective-permute-done.5) | copy-start | bytes 786436
  90.4 2.8 %copy-start.8 = (bf16[4,32,1024]{2,1,0:T(8,128)(2,1)}, bf16[4,32,1024]{2,1,0:T(8,128)(2,1)S(1)}, u32[]{:S(2)}) copy-start(bf16[4,32,1024]{2,1,0:T(8,128)(2,1)S(1)} %collective-permute-done.4) | copy-start | bytes 786436
  90.4 2.7 %copy-start.9 = (bf16[4,32,1024]{2,1,0:T(8,128)(2,1)}, bf16[4,32,1024]{2,1,0:T(8,128)(2,1)S(1)}, u32[]{:S(2)}) copy-start(bf16[4,32,1024]{2,1,0:T(8,128)(2,1)S(1)} %collective-permute-done.3) | copy-start | bytes 786436
  90.4 2.7 %collective-permute-start.6 = (bf16[16,2,8,2048]{3,2,1,0:T(8,128)(2,1)S(1)}, bf16[16,2,8,2048]{3,2,1,0:T(8,128)(2,1)S(1)}, u32[]{:S(2)}, u32[]{:S(2)}) collective-permute-start(bf16[16,2,8,2048]{3,2,1,0:T(8,128)(2,1)S(1)} %get-tuple-element.51), channel_id=1, source_target_pairs={{0,1},{1,0},{2,3},{3,2},{4,5},{5,4},{6,7},{7,6},{8,9},{9,8},{10,11... | collective-permute-start | bytes 3145736 | tf_op jit(solution)/shard_map/ppermute | solution.py:397
  94.6 10.6 %copy-start.10 = (f32[1024]{0:T(1024)S(1)}, f32[1024]{0:T(1024)}, u32[]{:S(2)}) copy-start(f32[1024]{0:T(1024)} %param.15) | copy-start | bytes 12292
  94.6 10.7 %slice-start = ((f32[1024]{0:T(1024)}), f32[256]{0:T(256)S(1)}, s32[]{:S(2)}) async-start(f32[1024]{0:T(1024)} %param.15), calls=%async_computation.4 | async-start | bytes 2048 | tf_op jit(solution)/shard_map/slice | solution.py:416
  94.6 10.7 %copy-start.11 = (f32[8]{0:T(128)S(1)}, f32[8]{0:T(128)}, u32[]{:S(2)}) copy-start(f32[8]{0:T(128)} %param.16) | copy-start | bytes 100
  94.6 13.4 %copy-start.5 = (bf16[64,8,2048]{2,1,0:T(8,128)(2,1)S(1)}, bf16[64,8,2048]{2,1,0:T(8,128)(2,1)}, u32[]{:S(2)}) copy-start(bf16[64,8,2048]{2,1,0:T(8,128)(2,1)} %get-tuple-element.34.refs_1_) | copy-start | bytes 6291460
  97.7 6.1 %copy-start.6 = (bf16[16,2,8,2048]{3,2,1,0:T(8,128)(2,1)}, bf16[16,2,8,2048]{3,2,1,0:T(8,128)(2,1)S(1)}, u32[]{:S(2)}) copy-start(bf16[16,2,8,2048]{3,2,1,0:T(8,128)(2,1)S(1)} %all-to-all-done.2.refs_5_) | copy-start | bytes 3145732
  97.7 29.1 %all-to-all-start.3 = ((bf16[16,2,8,2048]{3,2,1,0:T(8,128)(2,1)}), bf16[16,2,8,2048]{3,2,1,0:T(8,128)(2,1)}, u32[]{:S(2)}, u32[]{:S(2)}) async-start(bf16[16,2,8,2048]{3,2,1,0:T(8,128)(2,1)} %add_convert_fusion), calls=%async_computation.3 | async-start | bytes 2097152 | tf_op jit(solution)/shard_map/all_to_all | solution.py:367
  105.1 2.9 %collective-permute-start.7 = (bf16[1,16,32,1024]{3,2,1,0:T(8,128)(2,1)S(1)}, bf16[1,16,32,1024]{3,2,1,0:T(8,128)(2,1)}, u32[]{:S(2)}, u32[]{:S(2)}) collective-permute-start(bf16[1,16,32,1024]{3,2,1,0:T(8,128)(2,1)S(1)} %bitcast.25), channel_id=1, source_target_pairs={{0,1},{1,0},{2,3},{3,2},{4,5},{5,4},{6,7},{7,6},{8,9},{9,8},{10,11... | collective-permute-start | bytes 3145736 | tf_op jit(solution)/shard_map/ppermute | solution.py:339
  105.4 12.6 %copy-start.3 = (f32[8,1]{1,0:T(8,128)}, f32[8,1]{1,0:T(8,128)S(1)}, u32[]{:S(2)}) copy-start(f32[8,1]{1,0:T(8,128)S(1)} %copy.14.refs_4_) | copy-start | bytes 100
  105.7 12.3 %copy-start.2 = (f32[4,1,2048]{2,1,0:T(1,128)}, f32[4,1,2048]{2,1,0:T(1,128)S(1)}, u32[]{:S(2)}) copy-start(f32[4,1,2048]{2,1,0:T(1,128)S(1)} %broadcast_in_dim_reshape.6.refs_2_) | copy-start | bytes 98308
  107.5 10.5 %copy-start.1 = (f32[16,1,2048]{2,1,0:T(1,128)}, f32[16,1,2048]{2,1,0:T(1,128)S(1)}, u32[]{:S(2)}) copy-start(f32[16,1,2048]{2,1,0:T(1,128)S(1)} %tile.11.refs_3_) | copy-start | bytes 393220

commit v3 on v2

--- a/solution.py
+++ b/solution.py
@@ -186,12 +186,23 @@
 
 
 def cycle_kernel(
-    owners, parts, place_ref, tiles_ref, first_ref, second_ref, energy_ref, *rest
+    owners,
+    parts,
+    chunks,
+    place_ref,
+    out_tiles_ref,
+    tiles_ref,
+    early_ref,
+    first_ref,
+    rows_ref,
+    energy_ref,
+    *rest,
 ):
-    pieces, (base_ref, dress, wide, rows) = rest[:-4], rest[-4:]
+    pieces, (base_ref, dress, wide, rows, sums, early_picks) = rest[:-6], rest[-6:]
+    size = VT * WA // owners // chunks
+    outer_tile = pl.program_id(0)
     groups = tiles_ref.shape[2] // LANES
     pairs = tiles_ref.shape[1]
-    outer_tile = pl.program_id(0)
 
     @pl.when(outer_tile == 0)
     def _():
@@ -240,87 +251,119 @@
                 axis=1,
             )
             b = outer + half
-            below = energy_ref[...] - first_ref[0] - second_ref[b]
-            base_ref[b] = tiles_ref[b].astype(jnp.float32) + cycle / below
-
-
-def cycle_terms(place, tiles, first, second, pair_energy, pieces, owners, parts):
+            below = energy_ref[...] - first_ref[0] - rows_ref[b : b + 1]
+            sums[b] = tiles_ref[b].astype(jnp.float32) + cycle / below
+
+    early = 0.0
+    if chunks > 1:
+        for owner in range(owners):
+            for slot in range(size):
+                tile = out_tiles_ref[owner * chunks * size + slot]
+                inside = jnp.where(lax.div(tile, VT) == outer_tile, 1.0, 0.0)
+                row = (owner * size + slot) * pairs
+                picked = selection(lax.rem(tile, VT), VT, pairs)
+                early_picks[row : row + pairs] = jnp.where(picked, inside, 0.0)
+        early = lax.dot_general(
+            early_picks[...].astype(early_ref.dtype),
+            early_ref[...],
+            (((0,), (0,)), ((), ())),
+            preferred_element_type=jnp.float32,
+        )
+    turned = jnp.swapaxes(sums[...], 0, 1)
+    for pair in range(pairs):
+        total = turned[pair]
+        if chunks > 1:
+            below = energy_ref[pair : pair + 1] - first_ref[0] - rows_ref[...]
+            total += early[pair * VT : (pair + 1) * VT] / below
+        base_ref[pair] = total.astype(base_ref.dtype)
+
+
+def cycle_terms(place, out_tiles, tiles, early, first, rows, pair_energy, pieces, owners, parts, chunks):
     count, pairs, share = tiles.shape
     whole = lambda a: pl.BlockSpec(a.shape, lambda i, *_: (0,) * a.ndim)
     return pl.pallas_call(
-        lambda *refs: cycle_kernel(owners, parts, *refs),
-        out_shape=jax.ShapeDtypeStruct(tiles.shape, jnp.float32),
+        lambda *refs: cycle_kernel(owners, parts, chunks, *refs),
+        out_shape=jax.ShapeDtypeStruct((pairs, count, share), tiles.dtype),
         grid_spec=pltpu.PrefetchScalarGridSpec(
-            num_scalar_prefetch=1,
+            num_scalar_prefetch=2,
             grid=(WA,),
             in_specs=[
                 pl.BlockSpec((VT, pairs, share), lambda i, *_: (i, 0, 0)),
+                whole(early),
                 pl.BlockSpec((1, 1, share), lambda i, *_: (i, 0, 0)),
-                whole(second),
+                whole(rows),
                 whole(pair_energy),
             ]
             + [whole(piece) for piece in pieces],
-            out_specs=pl.BlockSpec((VT, pairs, share), lambda i, *_: (i, 0, 0)),
+            out_specs=pl.BlockSpec((pairs, VT, share), lambda i, *_: (0, i, 0)),
             scratch_shapes=[
                 pltpu.VMEM((VT * TILE, VT * TILE), jnp.float32),
                 pltpu.VMEM((VT * LANES, VT * LANES), tiles.dtype),
                 pltpu.VMEM((pairs * share // LANES, VT * LANES), tiles.dtype),
-            ],
-        ),
-        compiler_params=pltpu.CompilerParams(vmem_limit_bytes=48 * MIB),
+                pltpu.VMEM((VT, pairs, share), jnp.float32),
+                pltpu.VMEM((early.shape[0], pairs * VT), jnp.float32),
+            ],
+        ),
+        compiler_params=pltpu.CompilerParams(vmem_limit_bytes=36 * MIB),
         cost_estimate=pl.CostEstimate(
             flops=4 * count * pairs * share * VT * TILE,
             bytes_accessed=8 * count * pairs * share,
             transcendentals=0,
         ),
-    )(place, tiles, first, second, pair_energy, *pieces)
+    )(place, out_tiles, tiles, early, first, rows, pair_energy, *pieces)
 
 
 def finish_kernel(
-    chunks, out_tiles_ref, base_ref, first_ref, second_ref, energy_ref, *rest
+    owners, chunks, out_tiles_ref, energy_ref, base_ref, first_ref, rows_ref, last_ref, out_ref, *scratch
 ):
-    parts, out_ref, sums = rest[:chunks], rest[-2], rest[-1]
-    for chunk, part in enumerate(parts):
-        owners, size = part.shape[:2]
+    turned_ref, picks_ref = scratch
+    pairs, count, width = out_ref.shape
+    span = pl.ds(pl.multiple_of(pl.program_id(0) * width, width), width)
+    size = count // owners // chunks
+
+    @pl.when(pl.program_id(0) == 0)
+    def _():
         for owner in range(owners):
             for slot in range(size):
-                tile = out_tiles_ref[(owner * chunks + chunk) * size + slot]
-                below = (
-                    energy_ref[...] - first_ref[lax.div(tile, VT)] - second_ref[lax.rem(tile, VT)]
-                )
-                sums[tile] = base_ref[tile] + part[owner, slot].astype(jnp.float32) / below
-    out_ref[...] = jnp.swapaxes(sums[...], 0, 1).astype(out_ref.dtype)
-
-
-def finish(out_tiles, base, first, second, pair_energy, parts, dtype):
-    count, pairs, share = base.shape
-    width = min(share, 1024)
+                tile = out_tiles_ref[((owner + 1) * chunks - 1) * size + slot]
+                row = (owner * size + slot) * pairs
+                picked = selection(tile, count, pairs)
+                turned_ref[row : row + pairs] = jnp.where(picked, 1.0, 0.0)
+        picks_ref[...] = turned_ref[...].T.astype(picks_ref.dtype)
+
+    ladder = jnp.dot(picks_ref[...], last_ref[:, span], preferred_element_type=jnp.float32)
+    for pair in range(pairs):
+        for outer in range(count // VT):
+            inner = slice(outer * VT, (outer + 1) * VT)
+            below = energy_ref[pair] - first_ref[outer, :, span] - rows_ref[:, span]
+            start = pair * count + outer * VT
+            term = ladder[start : start + VT] / below
+            out_ref[pair, inner] = (base_ref[pair, inner, span].astype(jnp.float32) + term).astype(
+                out_ref.dtype
+            )
+
+
+def finish(out_tiles, base, first, rows, pair_energy, last, owners, chunks):
+    pairs, count, share = base.shape
+    width = min(share, 512)
     return pl.pallas_call(
-        lambda *refs: finish_kernel(len(parts), *refs),
-        out_shape=jax.ShapeDtypeStruct((pairs, count, share), dtype),
-        grid_spec=pltpu.PrefetchScalarGridSpec(
-            num_scalar_prefetch=1,
-            grid=(share // width,),
-            in_specs=[
-                pl.BlockSpec((count, pairs, width), lambda i, _: (0, 0, i)),
-                pl.BlockSpec((WA, 1, width), lambda i, _: (0, 0, i)),
-                pl.BlockSpec((VT, 1, width), lambda i, _: (0, 0, i)),
-                pl.BlockSpec((pairs, 1), lambda i, _: (0, 0)),
-            ]
-            + [
-                pl.BlockSpec(part.shape[:2] + (pairs, width), lambda i, _: (0, 0, 0, i))
-                for part in parts
-            ],
-            out_specs=pl.BlockSpec((pairs, count, width), lambda i, _: (0, 0, i)),
-            scratch_shapes=[pltpu.VMEM((count, pairs, width), jnp.float32)],
-        ),
-        compiler_params=pltpu.CompilerParams(vmem_limit_bytes=56 * MIB),
+        lambda *refs: finish_kernel(owners, chunks, *refs),
+        out_shape=jax.ShapeDtypeStruct((pairs, count, share), base.dtype),
+        grid=(share // width,),
+        in_specs=[pl.BlockSpec(memory_space=pltpu.SMEM)] * 2
+        + [pl.BlockSpec(memory_space=pltpu.VMEM)] * 4,
+        out_specs=pl.BlockSpec((pairs, count, width), lambda i: (0, 0, i)),
+        scratch_shapes=[
+            pltpu.VMEM((last.shape[0], pairs * count), jnp.float32),
+            pltpu.VMEM((pairs * count, last.shape[0]), base.dtype),
+        ],
+        compiler_params=pltpu.CompilerParams(vmem_limit_bytes=16 * MIB),
         cost_estimate=pl.CostEstimate(
             flops=8 * count * pairs * share,
-            bytes_accessed=8 * count * pairs * share,
+            bytes_accessed=6 * count * pairs * share,
             transcendentals=0,
         ),
-    )(out_tiles, base, first, second, pair_energy, *parts)
+    )(out_tiles, pair_energy, base, first, rows, last)
 
 
 def exchanges(axis, size, radices):
@@ -371,6 +414,10 @@
         steps = exchanges("pair", owners, [2, 2])
         gathered = [lax.dynamic_slice_in_dim(dressing, int_index * own, own, 0)[None]]
         together = lax.optimization_barrier
+        energies = vir_energy.reshape(VT, TILE)
+        own_energy = lax.dynamic_slice_in_dim(energies[:WA], int_index * strip, strip, 1)
+        first = jnp.repeat(own_energy, TILE, axis=1)[:, None]
+        second = jnp.tile(energies, (1, strip))
         received, returned = [], []
         if steps:
             gathered = exchange(joined(gathered), steps.pop(0))
@@ -383,7 +430,9 @@
             if c == 0 and steps:
                 gathered = exchange(joined(gathered), steps.pop(0))
             if c == 0:
-                received[c], gathered = together((received[c], gathered))
+                received[c], gathered, first, second = together(
+                    (received[c], gathered, first, second)
+                )
             if c == 0 and steps:
                 gathered = exchange(joined(gathered), steps.pop(0))
             terms = ladder(
@@ -412,14 +461,25 @@
         for step in exchanges("int", parts, []):
             pieces = exchange(joined(pieces), step)
 
-        energies = vir_energy.reshape(VT, TILE)
-        own_energy = lax.dynamic_slice_in_dim(energies[:WA], int_index * strip, strip, 1)
-        first = jnp.repeat(own_energy, TILE, axis=1)[:, None]
-        second = jnp.tile(energies, (1, strip))[:, None]
         energy = pair_energy[:, None]
         place = jnp.stack([lax.axis_index("pair"), int_index]).astype(jnp.int32)
-        base = cycle_terms(place, masked, first, second, energy, pieces, owners, parts)
-        return finish(out_tiles, base, first, second, energy, returned, amps.dtype)
+        flat = [part.reshape(owners * size * pairs, share) for part in returned]
+        base = cycle_terms(
+            place,
+            out_tiles,
+            masked,
+            flat[0],
+            first,
+            second,
+            energy,
+            pieces,
+            owners,
+            parts,
+            chunks,
+        )
+        return finish(
+            out_tiles, base, first, second, pair_energy, flat[-1], owners, chunks
+        )
 
     in_specs = (
         P("pair", None, "int"),

time: 133 us -> 131 us (0.985)
  local copies, waits for them, and re-layouts: 3.29 us -> 8.79 us
  waiting for transfers between devices: 35 us -> 29.9 us
  Pallas kernels: 55.3 us -> 52.4 us
    unnamed x24 -> x30, local copies, waits for them, and re-layouts: 0.95 us -> 8.16 us
    all_to_all x4, waiting for transfers between devices: 32 us -> 25.7 us  [exchanged(): return lax.all_to_all(part, 'pair', split_axis=0, concat_axis=0, tiled=True)]
    pallas_call x2, Pallas kernels: 15.8 us -> 12.8 us  [the longest x1 9.37 us: cycle_terms(): pl.pallas_call(lambda *refs: cycle_kernel(owners, parts, chunks, *refs),...]
    another operation x3, local copies, waits for them, and re-layouts: 1.91 us -> 0.21 us  [shards(): second = jnp.tile(energies, (1, strip))]
  transfers between devices with their start and end apart: 12 -> 12, of which waited for: 6 -> 6; matrix products, arithmetic and copies ran while one was open for 5% -> 4% of each run, Pallas kernels for 37% -> 38%
where the time goes in v3:
time: 131 us; the launch traced here: 130 us
  Pallas kernels  52.4 us (40%)
  starting transfers between devices  34.6 us (26%)
  waiting for transfers between devices  29.9 us (23%)
  local copies, waits for them, and re-layouts  8.79 us (7%)
  other arithmetic  4.17 us (3%)
    pallas_call x2, Pallas kernels, ladder(): pl.pallas_call(lambda *refs: ladder_kernel(first_slot, *refs), out_shape=...  31.4 us
    all_to_all x4, waiting for transfers between devices, exchanged(): return lax.all_to_all(part, 'pair', split_axis=0, concat_axis=0, tiled=True)  25.7 us
    all_to_all x4, starting transfers between devices, exchanged(): return lax.all_to_all(part, 'pair', split_axis=0, concat_axis=0, tiled=True)  24.7 us
    ppermute x6, starting transfers between devices, exchange(): lax.ppermute(block, axis, [(j, j ^ distance) for j in range(size)])  9.71 us
    pallas_call x1, Pallas kernels, cycle_terms(): pl.pallas_call(lambda *refs: cycle_kernel(owners, parts, chunks, *refs),...  9.37 us
    unnamed x30, local copies, waits for them, and re-layouts  8.16 us
    pallas_call x1, Pallas kernels, prepare(): pl.pallas_call(lambda *refs: prepare_kernel(owners, chunks, *refs), out_s...  4.5 us
    pallas_call x1, Pallas kernels, prepare_first(): pl.pallas_call(lambda *refs: first_kernel(chunks, *refs), out_shape=jax.S...  3.75 us
  transfers between devices with their start and end apart: 12, of which 6 were waited for; matrix products, arithmetic and copies ran while one was open for 4% of the time, Pallas kernels for 38%

profile of v3, /device:TPU:0, one launch (start us, length us, event | category | flops | bytes accessed | tf_op | source)
XLA Modules:
  0.0 130.1 jit_solution(6740833036340729400)
XLA Ops:
  0.0 0.0 copy-start
  0.0 0.9 copy-done
  0.9 0.0 copy-start.14
  0.9 0.0 slice-start
  0.9 4.1 %collective-permute-start = (bf16[1,32,1024]{2,1,0:T(8,128)(2,1)S(1)}, bf16[1,32,1024]{2,1,0:T(8,128)(2,1)S(1)}, u32[]{:S(2)}, u32[]{:S(2)}) collective-permute-start(bf16[1,32,1024]{2,1,0:T(8,128)(2,1)S(1)} %dynamic-slice_bitcast_fusion), channel_id=1, source_target_pairs={{0,16},{2,18},{4,20},{6,22},{8,24},{10,26},{12,28},{14,30},{16,0},... | collective-permute-start | bytes 196616 | tf_op jit(solution)/shard_map/ppermute | solution.py:382
  5.0 3.8 %shard_map.92 = bf16[16,2,8,2048]{3,2,1,0:T(8,128)(2,1)} custom-call(s32[64]{0:T(128)} %refs_0_.4, bf16[8,64,2048]{2,1,0:T(8,128)(2,1)} %refs_1_.7, s32[8,64]{1,0:T(8,128)} %refs_2_.3), custom_call_target="tpu_custom_call" | custom-call | flops 536870912 | bytes 3145728 | tf_op jit(solution)/shard_map/pallas_call | solution.py:44
  8.8 0.0 collective-permute-done
  8.8 6.5 %all-to-all-start = ((bf16[16,2,8,2048]{3,2,1,0:T(8,128)(2,1)}), bf16[16,2,8,2048]{3,2,1,0:T(8,128)(2,1)S(1)}, u32[]{:S(2)}, u32[]{:S(2)}) async-start(bf16[16,2,8,2048]{3,2,1,0:T(8,128)(2,1)} %shard_map.92), calls=%async_computation | async-start | bytes 2097152 | tf_op jit(solution)/shard_map/all_to_all | solution.py:410
  15.4 2.0 %collective-permute-start.1 = (bf16[2,32,1024]{2,1,0:T(8,128)(2,1)S(1)}, bf16[2,32,1024]{2,1,0:T(8,128)(2,1)S(1)}, u32[]{:S(2)}, u32[]{:S(2)}) collective-permute-start(bf16[2,32,1024]{2,1,0:T(8,128)(2,1)S(1)} %maximum_bitcast_fusion), channel_id=1, source_target_pairs={{0,8},{2,10},{4,12},{6,14},{8,0},{10,2},{12,4},{14,6},{16,24},{18,... | collective-permute-start | bytes 393224 | tf_op jit(solution)/shard_map/ppermute | solution.py:382
  17.3 0.0 copy-done.14
  17.3 0.1 tile.10
  17.4 0.0 slice-done
  17.4 0.1 slice.15
  17.5 0.1 constant_dynamic-slice_fusion
  17.6 0.1 broadcast_in_dim.12
  17.6 0.1 broadcast_in_dim_reshape.6.refs_4_.refs_3_
  17.8 0.1 tile.12.refs_5_.refs_4_
  17.9 4.5 %shard_map.91 = (bf16[64,8,2048]{2,1,0:T(8,128)(2,1)}, bf16[16,2,8,2048]{3,2,1,0:T(8,128)(2,1)}) custom-call(s32[64]{0:T(128)} %refs_0_.4, bf16[8,64,2048]{2,1,0:T(8,128)(2,1)} %refs_1_.7, s32[8,64]{1,0:T(8,128)} %refs_2_.3), custom_call_target="tpu_custom_call" | custom-call | flops 2097152 | bytes 6291456 | tf_op jit(solution)/shard_map/pallas_call | solution.py:84
  22.4 17.2 %all-to-all-done.refs_2_ = bf16[16,2,8,2048]{3,2,1,0:T(8,128)(2,1)S(1)} async-done(((bf16[16,2,8,2048]{3,2,1,0:T(8,128)(2,1)}), bf16[16,2,8,2048]{3,2,1,0:T(8,128)(2,1)S(1)}, u32[]{:S(2)}, u32[]{:S(2)}) %all-to-all-start) | async-done | bytes 1048608 | tf_op jit(solution)/shard_map/all_to_all | solution.py:410
  39.6 0.0 collective-permute-done.1
  39.6 5.8 %all-to-all-start.1 = ((bf16[16,2,8,2048]{3,2,1,0:T(8,128)(2,1)}), bf16[16,2,8,2048]{3,2,1,0:T(8,128)(2,1)S(1)}, u32[]{:S(2)}, u32[]{:S(2)}) async-start(bf16[16,2,8,2048]{3,2,1,0:T(8,128)(2,1)} %get-tuple-element.39), calls=%async_computation.1 | async-start | bytes 2097152 | tf_op jit(solution)/shard_map/all_to_all | solution.py:410
  45.4 0.0 copy-done.6
  45.4 15.7 %shard_map.93 = (bf16[16,2,8,2048]{3,2,1,0:T(8,128)(2,1)S(1)}, bf16[16,2,8,2048]{3,2,1,0:T(8,128)(2,1)S(1)}) custom-call(s32[1]{0:T(128)} %bitcast.1.refs_0_, s32[4]{0:T(128)S(1)} %copy-done.6, bf16[16,2,8,2048]{3,2,1,0:T(8,128)(2,1)S(1)} %all-to-all-done.refs_2_, bf16[4,4096,2048]{2,1,0:T(8,128)(2,1)} %refs_3_.3), custom_call_target="tpu_custom_call" | custom-call | flops 4294967296 | bytes 33554432 | tf_op jit(solution)/shard_map/pallas_call | solution.py:156
  61.1 0.1 collective-permute-start.2
  61.3 0.0 copy-start.11
  61.3 2.9 %collective-permute-start.5 = (bf16[4,32,1024]{2,1,0:T(8,128)(2,1)S(1)}, bf16[4,32,1024]{2,1,0:T(8,128)(2,1)S(1)}, u32[]{:S(2)}, u32[]{:S(2)}) collective-permute-start(bf16[4,32,1024]{2,1,0:T(8,128)(2,1)S(1)} %bitcast.32), channel_id=1, source_target_pairs={{0,6},{2,4},{4,2},{6,0},{8,14},{10,12},{12,10},{14,8},{16,22},{18,... | collective-permute-start | bytes 786440 | tf_op jit(solution)/shard_map/ppermute | solution.py:382
  64.2 0.6 collective-permute-start.4
  64.7 0.1 collective-permute-start.3
  64.8 0.0 collective-permute-done.2
  64.8 1.4 %add_convert_fusion.1 = bf16[16,2,8,2048]{3,2,1,0:T(8,128)(2,1)} fusion(bf16[16,2,8,2048]{3,2,1,0:T(8,128)(2,1)S(1)} %collective-permute-done.2, bf16[16,2,8,2048]{3,2,1,0:T(8,128)(2,1)S(1)} %get-tuple-element.44), kind=kLoop, calls=%fused_computation.1 | loop fusion | flops 2097152 | bytes 3145728 | tf_op jit(solution)/shard_map/convert_element_type | solution.py:450
  66.2 2.3 %all-to-all-done.1.refs_2_ = bf16[16,2,8,2048]{3,2,1,0:T(8,128)(2,1)S(1)} async-done(((bf16[16,2,8,2048]{3,2,1,0:T(8,128)(2,1)}), bf16[16,2,8,2048]{3,2,1,0:T(8,128)(2,1)S(1)}, u32[]{:S(2)}, u32[]{:S(2)}) %all-to-all-start.1) | async-done | bytes 1048608 | tf_op jit(solution)/shard_map/all_to_all | solution.py:410
  68.4 6.3 %all-to-all-start.2 = ((bf16[16,2,8,2048]{3,2,1,0:T(8,128)(2,1)}), bf16[16,2,8,2048]{3,2,1,0:T(8,128)(2,1)S(1)}, u32[]{:S(2)}, u32[]{:S(2)}) async-start(bf16[16,2,8,2048]{3,2,1,0:T(8,128)(2,1)} %add_convert_fusion.1), calls=%async_computation.2 | async-start | bytes 2097152 | tf_op jit(solution)/shard_map/all_to_all | solution.py:410
  74.7 15.7 %shard_map.94 = (bf16[16,2,8,2048]{3,2,1,0:T(8,128)(2,1)S(1)}, bf16[16,2,8,2048]{3,2,1,0:T(8,128)(2,1)S(1)}) custom-call(s32[1]{0:T(128)} %bitcast.1.refs_0_, s32[4]{0:T(128)S(1)} %copy-done.6, bf16[16,2,8,2048]{3,2,1,0:T(8,128)(2,1)S(1)} %all-to-all-done.1.refs_2_, bf16[4,4096,2048]{2,1,0:T(8,128)(2,1)} %refs_3_.3), custom_call_target="tpu_custom_call" | custom-call | flops 4294967296 | bytes 33554432 | tf_op jit(solution)/shard_map/pallas_call | solution.py:156
  90.5 0.0 copy-done.11
  90.5 0.0 collective-permute-done.5
  90.5 0.0 copy-start.12
  90.5 0.0 collective-permute-done.4
  90.5 0.0 copy-start.13
  90.5 0.0 collective-permute-done.3
  90.5 0.1 collective-permute-start.6
  90.6 2.6 %collective-permute-done.6 = bf16[16,2,8,2048]{3,2,1,0:T(8,128)(2,1)S(1)} collective-permute-done((bf16[16,2,8,2048]{3,2,1,0:T(8,128)(2,1)S(1)}, bf16[16,2,8,2048]{3,2,1,0:T(8,128)(2,1)S(1)}, u32[]{:S(2)}, u32[]{:S(2)}) %collective-permute-start.6) | collective-permute-done | bytes 1048608 | tf_op jit(solution)/shard_map/ppermute | solution.py:446
  93.2 1.4 %add_convert_fusion = bf16[16,2,8,2048]{3,2,1,0:T(8,128)(2,1)} fusion(bf16[16,2,8,2048]{3,2,1,0:T(8,128)(2,1)S(1)} %collective-permute-done.6, bf16[16,2,8,2048]{3,2,1,0:T(8,128)(2,1)S(1)} %get-tuple-element.52), kind=kLoop, calls=%fused_computation | loop fusion | flops 2097152 | bytes 3145728 | tf_op jit(solution)/shard_map/convert_element_type | solution.py:450
  94.6 3.1 %all-to-all-done.2 = bf16[16,2,8,2048]{3,2,1,0:T(8,128)(2,1)S(1)} async-done(((bf16[16,2,8,2048]{3,2,1,0:T(8,128)(2,1)}), bf16[16,2,8,2048]{3,2,1,0:T(8,128)(2,1)S(1)}, u32[]{:S(2)}, u32[]{:S(2)}) %all-to-all-start.2) | async-done | bytes 1048608 | tf_op jit(solution)/shard_map/all_to_all | solution.py:410
  97.8 0.0 copy-done.12
  97.8 0.0 copy-done.13
  97.8 6.1 %all-to-all-start.3 = ((bf16[16,2,8,2048]{3,2,1,0:T(8,128)(2,1)}), bf16[16,2,8,2048]{3,2,1,0:T(8,128)(2,1)S(1)}, u32[]{:S(2)}, u32[]{:S(2)}) async-start(bf16[16,2,8,2048]{3,2,1,0:T(8,128)(2,1)} %add_convert_fusion), calls=%async_computation.3 | async-start | bytes 2097152 | tf_op jit(solution)/shard_map/all_to_all | solution.py:410
  103.8 1.3 %pad_maximum_fusion = bf16[4,4,32,1024]{3,2,1,0:T(8,128)(2,1)S(1)} fusion(bf16[4,1,32,1024]{3,2,1,0:T(8,128)(2,1)} %bitcast.38, bf16[4,1,32,1024]{3,2,1,0:T(8,128)(2,1)} %bitcast.39, bf16[4,1,32,1024]{3,2,1,0:T(8,128)(2,1)} %bitcast.15, bf16[4,1,32,1024]{3,2,1,0:T(8,128)(2,1)} %bitcast.35), kind=kLoop, calls=%fused_computation.2 | loop fusion | flops 1572864 | bytes 2097152 | tf_op jit(solution)/shard_map/stack | solution.py:389
  105.2 0.0 copy-done.1
  105.2 0.1 collective-permute-start.7
  105.3 0.0 copy-start.3
  105.3 1.0 copy-done.3
  106.3 0.0 copy-done.5
  106.3 0.1 copy.14.refs_6_
  106.3 0.1 pad_add_fusion.refs_0_
  106.4 1.5 %collective-permute-done.7.refs_8_ = bf16[1,16,32,1024]{3,2,1,0:T(8,128)(2,1)S(1)} collective-permute-done((bf16[1,16,32,1024]{3,2,1,0:T(8,128)(2,1)S(1)}, bf16[1,16,32,1024]{3,2,1,0:T(8,128)(2,1)S(1)}, u32[]{:S(2)}, u32[]{:S(2)}) %collective-permute-start.7) | collective-permute-done | bytes 1048608 | tf_op jit(solution)/shard_map/ppermute | solution.py:382
  107.9 1.0 copy-done.9
  108.9 0.0 copy-done.7
  108.9 1.2 copy-done.2
  110.1 1.2 copy-done.4
  111.3 1.6 %copy-done.8 = bf16[64,8,2048]{2,1,0:T(8,128)(2,1)S(1)} copy-done((bf16[64,8,2048]{2,1,0:T(8,128)(2,1)S(1)}, bf16[64,8,2048]{2,1,0:T(8,128)(2,1)}, u32[]{:S(2)}) %copy-start.8) | copy-done | bytes 2097176
  112.9 1.2 copy-done.10
  114.2 9.4 %shard_map.95.refs_2_ = bf16[8,64,2048]{2,1,0:T(8,128)(2,1)S(1)} custom-call(s32[2]{0:T(128)S(1)} %pad_add_fusion.refs_0_, s32[64]{0:T(128)S(1)} %copy-done.7, bf16[64,8,2048]{2,1,0:T(8,128)(2,1)S(1)} %copy-done.8, bf16[256,2048]{1,0:T(8,128)(2,1)S(1)} %bitcast.28, f32[4,1,2048]{2,1,0:T(1,128)S(1)} %broadcast_in_dim_reshape.6.refs_4_.refs_3_, ...), custom_call_target="tpu_custom_call" | custom-call | flops 4294967296 | bytes 8388608 | tf_op jit(solution)/shard_map/pallas_call | solution.py:284
  123.5 3.1 %all-to-all-done.3 = bf16[16,2,8,2048]{3,2,1,0:T(8,128)(2,1)S(1)} async-done(((bf16[16,2,8,2048]{3,2,1,0:T(8,128)(2,1)}), bf16[16,2,8,2048]{3,2,1,0:T(8,128)(2,1)S(1)}, u32[]{:S(2)}, u32[]{:S(2)}) %all-to-all-start.3) | async-done | bytes 1048608 | tf_op jit(solution)/shard_map/all_to_all | solution.py:410
  126.7 3.4 %shard_map.96 = bf16[8,64,2048]{2,1,0:T(8,128)(2,1)} custom-call(s32[64]{0:T(128)S(1)} %copy-done.7, f32[8]{0:T(128)S(1)} %copy-done.5, bf16[8,64,2048]{2,1,0:T(8,128)(2,1)S(1)} %shard_map.95.refs_2_, f32[4,1,2048]{2,1,0:T(1,128)S(1)} %broadcast_in_dim_reshape.6.refs_4_.refs_3_, f32[16,2048]{1,0:T(8,128)S(1)} %tile.12.refs_5_.refs_4_, ...), custom_call_target="tpu_custom_call" | custom-call | flops 8388608 | bytes 6291456 | tf_op jit(solution)/shard_map/pallas_call | solution.py:349
  (13 shorter events, 0.1 us)
Async XLA Ops:
  0.0 0.9 copy-start
  0.9 16.4 %copy-start.14 = (f32[1024]{0:T(1024)S(1)}, f32[1024]{0:T(1024)}, u32[]{:S(2)}) copy-start(f32[1024]{0:T(1024)} %param.15) | copy-start | bytes 12292
  0.9 16.5 %slice-start = ((f32[1024]{0:T(1024)}), f32[256]{0:T(256)S(1)}, s32[]{:S(2)}) async-start(f32[1024]{0:T(1024)} %param.15), calls=%async_computation.4 | async-start | bytes 2048 | tf_op jit(solution)/shard_map/slice | solution.py:418
  0.9 7.9 %collective-permute-start = (bf16[1,32,1024]{2,1,0:T(8,128)(2,1)S(1)}, bf16[1,32,1024]{2,1,0:T(8,128)(2,1)S(1)}, u32[]{:S(2)}, u32[]{:S(2)}) collective-permute-start(bf16[1,32,1024]{2,1,0:T(8,128)(2,1)S(1)} %dynamic-slice_bitcast_fusion), channel_id=1, source_target_pairs={{0,16},{2,18},{4,20},{6,22},{8,24},{10,26},{12,28},{14,30},{16,0},... | collective-permute-start | bytes 196616 | tf_op jit(solution)/shard_map/ppermute | solution.py:382
  8.8 30.8 %all-to-all-start = ((bf16[16,2,8,2048]{3,2,1,0:T(8,128)(2,1)}), bf16[16,2,8,2048]{3,2,1,0:T(8,128)(2,1)S(1)}, u32[]{:S(2)}, u32[]{:S(2)}) async-start(bf16[16,2,8,2048]{3,2,1,0:T(8,128)(2,1)} %shard_map.92), calls=%async_computation | async-start | bytes 2097152 | tf_op jit(solution)/shard_map/all_to_all | solution.py:410
  15.4 24.2 %collective-permute-start.1 = (bf16[2,32,1024]{2,1,0:T(8,128)(2,1)S(1)}, bf16[2,32,1024]{2,1,0:T(8,128)(2,1)S(1)}, u32[]{:S(2)}, u32[]{:S(2)}) collective-permute-start(bf16[2,32,1024]{2,1,0:T(8,128)(2,1)S(1)} %maximum_bitcast_fusion), channel_id=1, source_target_pairs={{0,8},{2,10},{4,12},{6,14},{8,0},{10,2},{12,4},{14,6},{16,24},{18,... | collective-permute-start | bytes 393224 | tf_op jit(solution)/shard_map/ppermute | solution.py:382
  17.9 27.5 %copy-start.6 = (s32[4]{0:T(128)S(1)}, s32[4]{0:T(128)}, u32[]{:S(2)}) copy-start(s32[4]{0:T(128)} %refs_1_.9) | copy-start | bytes 52
  39.6 28.8 %all-to-all-start.1 = ((bf16[16,2,8,2048]{3,2,1,0:T(8,128)(2,1)}), bf16[16,2,8,2048]{3,2,1,0:T(8,128)(2,1)S(1)}, u32[]{:S(2)}, u32[]{:S(2)}) async-start(bf16[16,2,8,2048]{3,2,1,0:T(8,128)(2,1)} %get-tuple-element.39), calls=%async_computation.1 | async-start | bytes 2097152 | tf_op jit(solution)/shard_map/all_to_all | solution.py:410
  61.1 3.7 %collective-permute-start.2 = (bf16[16,2,8,2048]{3,2,1,0:T(8,128)(2,1)S(1)}, bf16[16,2,8,2048]{3,2,1,0:T(8,128)(2,1)S(1)}, u32[]{:S(2)}, u32[]{:S(2)}) collective-permute-start(bf16[16,2,8,2048]{3,2,1,0:T(8,128)(2,1)S(1)} %get-tuple-element.45), channel_id=1, source_target_pairs={{0,1},{1,0},{2,3},{3,2},{4,5},{5,4},{6,7},{7,6},{8,9},{9,8},{10,11... | collective-permute-start | bytes 3145736 | tf_op jit(solution)/shard_map/ppermute | solution.py:446
  61.3 29.2 %copy-start.11 = (bf16[2,2,32,1024]{3,2,1,0:T(8,128)(2,1)}, bf16[2,2,32,1024]{3,2,1,0:T(8,128)(2,1)S(1)}, u32[]{:S(2)}) copy-start(bf16[2,2,32,1024]{3,2,1,0:T(8,128)(2,1)S(1)} %pad_maximum_fusion.1) | copy-start | bytes 786436
  61.3 29.2 %collective-permute-start.5 = (bf16[4,32,1024]{2,1,0:T(8,128)(2,1)S(1)}, bf16[4,32,1024]{2,1,0:T(8,128)(2,1)S(1)}, u32[]{:S(2)}, u32[]{:S(2)}) collective-permute-start(bf16[4,32,1024]{2,1,0:T(8,128)(2,1)S(1)} %bitcast.32), channel_id=1, source_target_pairs={{0,6},{2,4},{4,2},{6,0},{8,14},{10,12},{12,10},{14,8},{16,22},{18,... | collective-permute-start | bytes 786440 | tf_op jit(solution)/shard_map/ppermute | solution.py:382
  64.2 26.3 %collective-permute-start.4 = (bf16[4,32,1024]{2,1,0:T(8,128)(2,1)S(1)}, bf16[4,32,1024]{2,1,0:T(8,128)(2,1)S(1)}, u32[]{:S(2)}, u32[]{:S(2)}) collective-permute-start(bf16[4,32,1024]{2,1,0:T(8,128)(2,1)S(1)} %bitcast.33), channel_id=1, source_target_pairs={{0,4},{2,6},{4,0},{6,2},{8,12},{10,14},{12,8},{14,10},{16,20},{18,... | collective-permute-start | bytes 786440 | tf_op jit(solution)/shard_map/ppermute | solution.py:382
  64.7 25.8 %collective-permute-start.3 = (bf16[4,32,1024]{2,1,0:T(8,128)(2,1)S(1)}, bf16[4,32,1024]{2,1,0:T(8,128)(2,1)}, u32[]{:S(2)}, u32[]{:S(2)}) collective-permute-start(bf16[4,32,1024]{2,1,0:T(8,128)(2,1)S(1)} %bitcast.34), channel_id=1, source_target_pairs={{0,2},{2,0},{4,6},{6,4},{8,10},{10,8},{12,14},{14,12},{16,18},{18,... | collective-permute-start | bytes 786440 | tf_op jit(solution)/shard_map/ppermute | solution.py:382
  68.4 29.3 %all-to-all-start.2 = ((bf16[16,2,8,2048]{3,2,1,0:T(8,128)(2,1)}), bf16[16,2,8,2048]{3,2,1,0:T(8,128)(2,1)S(1)}, u32[]{:S(2)}, u32[]{:S(2)}) async-start(bf16[16,2,8,2048]{3,2,1,0:T(8,128)(2,1)} %add_convert_fusion.1), calls=%async_computation.2 | async-start | bytes 2097152 | tf_op jit(solution)/shard_map/all_to_all | solution.py:410
  90.5 7.3 %copy-start.12 = (bf16[4,32,1024]{2,1,0:T(8,128)(2,1)}, bf16[4,32,1024]{2,1,0:T(8,128)(2,1)S(1)}, u32[]{:S(2)}) copy-start(bf16[4,32,1024]{2,1,0:T(8,128)(2,1)S(1)} %collective-permute-done.5) | copy-start | bytes 786436
  90.5 7.3 %copy-start.13 = (bf16[4,32,1024]{2,1,0:T(8,128)(2,1)}, bf16[4,32,1024]{2,1,0:T(8,128)(2,1)S(1)}, u32[]{:S(2)}) copy-start(bf16[4,32,1024]{2,1,0:T(8,128)(2,1)S(1)} %collective-permute-done.4) | copy-start | bytes 786436
  90.5 2.7 %collective-permute-start.6 = (bf16[16,2,8,2048]{3,2,1,0:T(8,128)(2,1)S(1)}, bf16[16,2,8,2048]{3,2,1,0:T(8,128)(2,1)S(1)}, u32[]{:S(2)}, u32[]{:S(2)}) collective-permute-start(bf16[16,2,8,2048]{3,2,1,0:T(8,128)(2,1)S(1)} %get-tuple-element.53), channel_id=1, source_target_pairs={{0,1},{1,0},{2,3},{3,2},{4,5},{5,4},{6,7},{7,6},{8,9},{9,8},{10,11... | collective-permute-start | bytes 3145736 | tf_op jit(solution)/shard_map/ppermute | solution.py:446
  94.6 11.6 %copy-start.5 = (f32[8]{0:T(128)S(1)}, f32[8]{0:T(128)}, u32[]{:S(2)}) copy-start(f32[8]{0:T(128)} %refs_1_.11) | copy-start | bytes 100
  94.6 14.3 %copy-start.7 = (s32[64]{0:T(128)S(1)}, s32[64]{0:T(128)}, u32[]{:S(2)}) copy-start(s32[64]{0:T(128)} %refs_0_.5) | copy-start | bytes 772
  97.8 7.4 %copy-start.1 = (bf16[16,2,8,2048]{3,2,1,0:T(8,128)(2,1)}, bf16[16,2,8,2048]{3,2,1,0:T(8,128)(2,1)S(1)}, u32[]{:S(2)}) copy-start(bf16[16,2,8,2048]{3,2,1,0:T(8,128)(2,1)S(1)} %all-to-all-done.2) | copy-start | bytes 3145732
  97.8 28.9 %all-to-all-start.3 = ((bf16[16,2,8,2048]{3,2,1,0:T(8,128)(2,1)}), bf16[16,2,8,2048]{3,2,1,0:T(8,128)(2,1)S(1)}, u32[]{:S(2)}, u32[]{:S(2)}) async-start(bf16[16,2,8,2048]{3,2,1,0:T(8,128)(2,1)} %add_convert_fusion), calls=%async_computation.3 | async-start | bytes 2097152 | tf_op jit(solution)/shard_map/all_to_all | solution.py:410
  105.2 2.7 %collective-permute-start.7 = (bf16[1,16,32,1024]{3,2,1,0:T(8,128)(2,1)S(1)}, bf16[1,16,32,1024]{3,2,1,0:T(8,128)(2,1)S(1)}, u32[]{:S(2)}, u32[]{:S(2)}) collective-permute-start(bf16[1,16,32,1024]{3,2,1,0:T(8,128)(2,1)S(1)} %bitcast.29), channel_id=1, source_target_pairs={{0,1},{1,0},{2,3},{3,2},{4,5},{5,4},{6,7},{7,6},{8,9},{9,8},{10,11... | collective-permute-start | bytes 3145736 | tf_op jit(solution)/shard_map/ppermute | solution.py:382
  105.3 1.0 copy-start.3
  107.9 1.0 copy-start.9
  108.9 1.2 copy-start.2
  110.1 1.2 copy-start.4
  111.3 1.6 %copy-start.8 = (bf16[64,8,2048]{2,1,0:T(8,128)(2,1)S(1)}, bf16[64,8,2048]{2,1,0:T(8,128)(2,1)}, u32[]{:S(2)}) copy-start(bf16[64,8,2048]{2,1,0:T(8,128)(2,1)} %get-tuple-element.36.refs_2_) | copy-start | bytes 6291460
  112.9 1.2 copy-start.10

commit v4 on v3

--- a/solution.py
+++ b/solution.py
@@ -345,7 +345,7 @@
 
 def finish(out_tiles, base, first, rows, pair_energy, last, owners, chunks):
     pairs, count, share = base.shape
-    width = min(share, 512)
+    width = min(share, 1024)
     return pl.pallas_call(
         lambda *refs: finish_kernel(owners, chunks, *refs),
         out_shape=jax.ShapeDtypeStruct((pairs, count, share), base.dtype),

time: 131 us -> 130 us (level)
  no operation moved by 1% of the time
where the time goes in v4:
time: 130 us
  Pallas kernels  51.8 us (40%)
  starting transfers between devices  34.6 us (27%)
  waiting for transfers between devices  29.9 us (23%)
  local copies, waits for them, and re-layouts  8.79 us (7%)
  other arithmetic  4.17 us (3%)
    pallas_call x2, Pallas kernels, ladder(): pl.pallas_call(lambda *refs: ladder_kernel(first_slot, *refs), out_shape=...  31.4 us
    all_to_all x4, waiting for transfers between devices, exchanged(): return lax.all_to_all(part, 'pair', split_axis=0, concat_axis=0, tiled=True)  25.7 us
    all_to_all x4, starting transfers between devices, exchanged(): return lax.all_to_all(part, 'pair', split_axis=0, concat_axis=0, tiled=True)  24.7 us
    ppermute x6, starting transfers between devices, exchange(): lax.ppermute(block, axis, [(j, j ^ distance) for j in range(size)])  9.71 us
    pallas_call x1, Pallas kernels, cycle_terms(): pl.pallas_call(lambda *refs: cycle_kernel(owners, parts, chunks, *refs),...  9.37 us
    unnamed x30, local copies, waits for them, and re-layouts  8.16 us
    pallas_call x1, Pallas kernels, prepare(): pl.pallas_call(lambda *refs: prepare_kernel(owners, chunks, *refs), out_s...  4.5 us
    pallas_call x1, Pallas kernels, prepare_first(): pl.pallas_call(lambda *refs: first_kernel(chunks, *refs), out_shape=jax.S...  3.75 us
  transfers between devices with their start and end apart: 12, of which 6 were waited for; matrix products, arithmetic and copies ran while one was open for 4% of the time, Pallas kernels for 38%

profile of v4, /device:TPU:0, one launch (start us, length us, event | category | flops | bytes accessed | tf_op | source)
XLA Modules:
  0.0 129.5 jit_solution(2557072872352628343)
XLA Ops:
  0.0 0.0 copy-start
  0.0 0.9 copy-done
  0.9 0.0 copy-start.14
  0.9 0.0 slice-start
  0.9 4.1 %collective-permute-start = (bf16[1,32,1024]{2,1,0:T(8,128)(2,1)S(1)}, bf16[1,32,1024]{2,1,0:T(8,128)(2,1)S(1)}, u32[]{:S(2)}, u32[]{:S(2)}) collective-permute-start(bf16[1,32,1024]{2,1,0:T(8,128)(2,1)S(1)} %dynamic-slice_bitcast_fusion), channel_id=1, source_target_pairs={{0,16},{2,18},{4,20},{6,22},{8,24},{10,26},{12,28},{14,30},{16,0},... | collective-permute-start | bytes 196616 | tf_op jit(solution)/shard_map/ppermute | solution.py:382
  5.0 3.8 %shard_map.92 = bf16[16,2,8,2048]{3,2,1,0:T(8,128)(2,1)} custom-call(s32[64]{0:T(128)} %refs_0_.4, bf16[8,64,2048]{2,1,0:T(8,128)(2,1)} %refs_1_.7, s32[8,64]{1,0:T(8,128)} %refs_2_.3), custom_call_target="tpu_custom_call" | custom-call | flops 536870912 | bytes 3145728 | tf_op jit(solution)/shard_map/pallas_call | solution.py:44
  8.8 0.0 collective-permute-done
  8.8 6.5 %all-to-all-start = ((bf16[16,2,8,2048]{3,2,1,0:T(8,128)(2,1)}), bf16[16,2,8,2048]{3,2,1,0:T(8,128)(2,1)S(1)}, u32[]{:S(2)}, u32[]{:S(2)}) async-start(bf16[16,2,8,2048]{3,2,1,0:T(8,128)(2,1)} %shard_map.92), calls=%async_computation | async-start | bytes 2097152 | tf_op jit(solution)/shard_map/all_to_all | solution.py:410
  15.4 2.0 %collective-permute-start.1 = (bf16[2,32,1024]{2,1,0:T(8,128)(2,1)S(1)}, bf16[2,32,1024]{2,1,0:T(8,128)(2,1)S(1)}, u32[]{:S(2)}, u32[]{:S(2)}) collective-permute-start(bf16[2,32,1024]{2,1,0:T(8,128)(2,1)S(1)} %maximum_bitcast_fusion), channel_id=1, source_target_pairs={{0,8},{2,10},{4,12},{6,14},{8,0},{10,2},{12,4},{14,6},{16,24},{18,... | collective-permute-start | bytes 393224 | tf_op jit(solution)/shard_map/ppermute | solution.py:382
  17.3 0.0 copy-done.14
  17.3 0.1 tile.10
  17.4 0.0 slice-done
  17.4 0.1 slice.15
  17.5 0.1 constant_dynamic-slice_fusion
  17.6 0.1 broadcast_in_dim.12
  17.6 0.1 broadcast_in_dim_reshape.6.refs_4_.refs_3_
  17.8 0.1 tile.12.refs_5_.refs_4_
  17.9 4.5 %shard_map.91 = (bf16[64,8,2048]{2,1,0:T(8,128)(2,1)}, bf16[16,2,8,2048]{3,2,1,0:T(8,128)(2,1)}) custom-call(s32[64]{0:T(128)} %refs_0_.4, bf16[8,64,2048]{2,1,0:T(8,128)(2,1)} %refs_1_.7, s32[8,64]{1,0:T(8,128)} %refs_2_.3), custom_call_target="tpu_custom_call" | custom-call | flops 2097152 | bytes 6291456 | tf_op jit(solution)/shard_map/pallas_call | solution.py:84
  22.4 17.2 %all-to-all-done.refs_2_ = bf16[16,2,8,2048]{3,2,1,0:T(8,128)(2,1)S(1)} async-done(((bf16[16,2,8,2048]{3,2,1,0:T(8,128)(2,1)}), bf16[16,2,8,2048]{3,2,1,0:T(8,128)(2,1)S(1)}, u32[]{:S(2)}, u32[]{:S(2)}) %all-to-all-start) | async-done | bytes 1048608 | tf_op jit(solution)/shard_map/all_to_all | solution.py:410
  39.6 0.0 collective-permute-done.1
  39.6 5.8 %all-to-all-start.1 = ((bf16[16,2,8,2048]{3,2,1,0:T(8,128)(2,1)}), bf16[16,2,8,2048]{3,2,1,0:T(8,128)(2,1)S(1)}, u32[]{:S(2)}, u32[]{:S(2)}) async-start(bf16[16,2,8,2048]{3,2,1,0:T(8,128)(2,1)} %get-tuple-element.39), calls=%async_computation.1 | async-start | bytes 2097152 | tf_op jit(solution)/shard_map/all_to_all | solution.py:410
  45.4 0.0 copy-done.6
  45.4 15.7 %shard_map.93 = (bf16[16,2,8,2048]{3,2,1,0:T(8,128)(2,1)S(1)}, bf16[16,2,8,2048]{3,2,1,0:T(8,128)(2,1)S(1)}) custom-call(s32[1]{0:T(128)} %bitcast.1.refs_0_, s32[4]{0:T(128)S(1)} %copy-done.6, bf16[16,2,8,2048]{3,2,1,0:T(8,128)(2,1)S(1)} %all-to-all-done.refs_2_, bf16[4,4096,2048]{2,1,0:T(8,128)(2,1)} %refs_3_.3), custom_call_target="tpu_custom_call" | custom-call | flops 4294967296 | bytes 33554432 | tf_op jit(solution)/shard_map/pallas_call | solution.py:156
  61.1 0.1 collective-permute-start.2
  61.3 0.0 copy-start.11
  61.3 2.9 %collective-permute-start.5 = (bf16[4,32,1024]{2,1,0:T(8,128)(2,1)S(1)}, bf16[4,32,1024]{2,1,0:T(8,128)(2,1)S(1)}, u32[]{:S(2)}, u32[]{:S(2)}) collective-permute-start(bf16[4,32,1024]{2,1,0:T(8,128)(2,1)S(1)} %bitcast.32), channel_id=1, source_target_pairs={{0,6},{2,4},{4,2},{6,0},{8,14},{10,12},{12,10},{14,8},{16,22},{18,... | collective-permute-start | bytes 786440 | tf_op jit(solution)/shard_map/ppermute | solution.py:382
  64.2 0.6 collective-permute-start.4
  64.7 0.1 collective-permute-start.3
  64.8 0.0 collective-permute-done.2
  64.8 1.4 %add_convert_fusion.1 = bf16[16,2,8,2048]{3,2,1,0:T(8,128)(2,1)} fusion(bf16[16,2,8,2048]{3,2,1,0:T(8,128)(2,1)S(1)} %collective-permute-done.2, bf16[16,2,8,2048]{3,2,1,0:T(8,128)(2,1)S(1)} %get-tuple-element.44), kind=kLoop, calls=%fused_computation.1 | loop fusion | flops 2097152 | bytes 3145728 | tf_op jit(solution)/shard_map/convert_element_type | solution.py:450
  66.2 2.3 %all-to-all-done.1.refs_2_ = bf16[16,2,8,2048]{3,2,1,0:T(8,128)(2,1)S(1)} async-done(((bf16[16,2,8,2048]{3,2,1,0:T(8,128)(2,1)}), bf16[16,2,8,2048]{3,2,1,0:T(8,128)(2,1)S(1)}, u32[]{:S(2)}, u32[]{:S(2)}) %all-to-all-start.1) | async-done | bytes 1048608 | tf_op jit(solution)/shard_map/all_to_all | solution.py:410
  68.4 6.3 %all-to-all-start.2 = ((bf16[16,2,8,2048]{3,2,1,0:T(8,128)(2,1)}), bf16[16,2,8,2048]{3,2,1,0:T(8,128)(2,1)S(1)}, u32[]{:S(2)}, u32[]{:S(2)}) async-start(bf16[16,2,8,2048]{3,2,1,0:T(8,128)(2,1)} %add_convert_fusion.1), calls=%async_computation.2 | async-start | bytes 2097152 | tf_op jit(solution)/shard_map/all_to_all | solution.py:410
  74.7 15.7 %shard_map.94 = (bf16[16,2,8,2048]{3,2,1,0:T(8,128)(2,1)S(1)}, bf16[16,2,8,2048]{3,2,1,0:T(8,128)(2,1)S(1)}) custom-call(s32[1]{0:T(128)} %bitcast.1.refs_0_, s32[4]{0:T(128)S(1)} %copy-done.6, bf16[16,2,8,2048]{3,2,1,0:T(8,128)(2,1)S(1)} %all-to-all-done.1.refs_2_, bf16[4,4096,2048]{2,1,0:T(8,128)(2,1)} %refs_3_.3), custom_call_target="tpu_custom_call" | custom-call | flops 4294967296 | bytes 33554432 | tf_op jit(solution)/shard_map/pallas_call | solution.py:156
  90.5 0.0 copy-done.11
  90.5 0.0 collective-permute-done.5
  90.5 0.0 copy-start.12
  90.5 0.0 collective-permute-done.4
  90.5 0.0 copy-start.13
  90.5 0.0 collective-permute-done.3
  90.5 0.1 collective-permute-start.6
  90.6 2.6 %collective-permute-done.6 = bf16[16,2,8,2048]{3,2,1,0:T(8,128)(2,1)S(1)} collective-permute-done((bf16[16,2,8,2048]{3,2,1,0:T(8,128)(2,1)S(1)}, bf16[16,2,8,2048]{3,2,1,0:T(8,128)(2,1)S(1)}, u32[]{:S(2)}, u32[]{:S(2)}) %collective-permute-start.6) | collective-permute-done | bytes 1048608 | tf_op jit(solution)/shard_map/ppermute | solution.py:446
  93.2 1.4 %add_convert_fusion = bf16[16,2,8,2048]{3,2,1,0:T(8,128)(2,1)} fusion(bf16[16,2,8,2048]{3,2,1,0:T(8,128)(2,1)S(1)} %collective-permute-done.6, bf16[16,2,8,2048]{3,2,1,0:T(8,128)(2,1)S(1)} %get-tuple-element.52), kind=kLoop, calls=%fused_computation | loop fusion | flops 2097152 | bytes 3145728 | tf_op jit(solution)/shard_map/convert_element_type | solution.py:450
  94.6 3.1 %all-to-all-done.2 = bf16[16,2,8,2048]{3,2,1,0:T(8,128)(2,1)S(1)} async-done(((bf16[16,2,8,2048]{3,2,1,0:T(8,128)(2,1)}), bf16[16,2,8,2048]{3,2,1,0:T(8,128)(2,1)S(1)}, u32[]{:S(2)}, u32[]{:S(2)}) %all-to-all-start.2) | async-done | bytes 1048608 | tf_op jit(solution)/shard_map/all_to_all | solution.py:410
  97.8 0.0 copy-done.12
  97.8 0.0 copy-done.13
  97.8 6.1 %all-to-all-start.3 = ((bf16[16,2,8,2048]{3,2,1,0:T(8,128)(2,1)}), bf16[16,2,8,2048]{3,2,1,0:T(8,128)(2,1)S(1)}, u32[]{:S(2)}, u32[]{:S(2)}) async-start(bf16[16,2,8,2048]{3,2,1,0:T(8,128)(2,1)} %add_convert_fusion), calls=%async_computation.3 | async-start | bytes 2097152 | tf_op jit(solution)/shard_map/all_to_all | solution.py:410
  103.8 1.3 %pad_maximum_fusion = bf16[4,4,32,1024]{3,2,1,0:T(8,128)(2,1)S(1)} fusion(bf16[4,1,32,1024]{3,2,1,0:T(8,128)(2,1)} %bitcast.38, bf16[4,1,32,1024]{3,2,1,0:T(8,128)(2,1)} %bitcast.39, bf16[4,1,32,1024]{3,2,1,0:T(8,128)(2,1)} %bitcast.15, bf16[4,1,32,1024]{3,2,1,0:T(8,128)(2,1)} %bitcast.35), kind=kLoop, calls=%fused_computation.2 | loop fusion | flops 1572864 | bytes 2097152 | tf_op jit(solution)/shard_map/stack | solution.py:389
  105.2 0.0 copy-done.1
  105.2 0.1 collective-permute-start.7
  105.3 0.0 copy-start.3
  105.3 1.0 copy-done.3
  106.3 0.0 copy-done.5
  106.3 0.1 copy.14.refs_6_
  106.3 0.1 pad_add_fusion.refs_0_
  106.4 1.5 %collective-permute-done.7.refs_8_ = bf16[1,16,32,1024]{3,2,1,0:T(8,128)(2,1)S(1)} collective-permute-done((bf16[1,16,32,1024]{3,2,1,0:T(8,128)(2,1)S(1)}, bf16[1,16,32,1024]{3,2,1,0:T(8,128)(2,1)S(1)}, u32[]{:S(2)}, u32[]{:S(2)}) %collective-permute-start.7) | collective-permute-done | bytes 1048608 | tf_op jit(solution)/shard_map/ppermute | solution.py:382
  107.9 1.0 copy-done.9
  108.9 0.0 copy-done.7
  108.9 1.2 copy-done.2
  110.1 1.2 copy-done.4
  111.3 1.6 %copy-done.8 = bf16[64,8,2048]{2,1,0:T(8,128)(2,1)S(1)} copy-done((bf16[64,8,2048]{2,1,0:T(8,128)(2,1)S(1)}, bf16[64,8,2048]{2,1,0:T(8,128)(2,1)}, u32[]{:S(2)}) %copy-start.8) | copy-done | bytes 2097176
  112.9 1.2 copy-done.10
  114.2 9.4 %shard_map.95.refs_2_ = bf16[8,64,2048]{2,1,0:T(8,128)(2,1)S(1)} custom-call(s32[2]{0:T(128)S(1)} %pad_add_fusion.refs_0_, s32[64]{0:T(128)S(1)} %copy-done.7, bf16[64,8,2048]{2,1,0:T(8,128)(2,1)S(1)} %copy-done.8, bf16[256,2048]{1,0:T(8,128)(2,1)S(1)} %bitcast.28, f32[4,1,2048]{2,1,0:T(1,128)S(1)} %broadcast_in_dim_reshape.6.refs_4_.refs_3_, ...), custom_call_target="tpu_custom_call" | custom-call | flops 4294967296 | bytes 8388608 | tf_op jit(solution)/shard_map/pallas_call | solution.py:284
  123.5 3.1 %all-to-all-done.3 = bf16[16,2,8,2048]{3,2,1,0:T(8,128)(2,1)S(1)} async-done(((bf16[16,2,8,2048]{3,2,1,0:T(8,128)(2,1)}), bf16[16,2,8,2048]{3,2,1,0:T(8,128)(2,1)S(1)}, u32[]{:S(2)}, u32[]{:S(2)}) %all-to-all-start.3) | async-done | bytes 1048608 | tf_op jit(solution)/shard_map/all_to_all | solution.py:410
  126.7 2.8 %shard_map.96 = bf16[8,64,2048]{2,1,0:T(8,128)(2,1)} custom-call(s32[64]{0:T(128)S(1)} %copy-done.7, f32[8]{0:T(128)S(1)} %copy-done.5, bf16[8,64,2048]{2,1,0:T(8,128)(2,1)S(1)} %shard_map.95.refs_2_, f32[4,1,2048]{2,1,0:T(1,128)S(1)} %broadcast_in_dim_reshape.6.refs_4_.refs_3_, f32[16,2048]{1,0:T(8,128)S(1)} %tile.12.refs_5_.refs_4_, ...), custom_call_target="tpu_custom_call" | custom-call | flops 8388608 | bytes 6291456 | tf_op jit(solution)/shard_map/pallas_call | solution.py:349
  (13 shorter events, 0.1 us)
Async XLA Ops:
  0.0 0.9 copy-start
  0.9 16.4 %copy-start.14 = (f32[1024]{0:T(1024)S(1)}, f32[1024]{0:T(1024)}, u32[]{:S(2)}) copy-start(f32[1024]{0:T(1024)} %param.15) | copy-start | bytes 12292
  0.9 16.5 %slice-start = ((f32[1024]{0:T(1024)}), f32[256]{0:T(256)S(1)}, s32[]{:S(2)}) async-start(f32[1024]{0:T(1024)} %param.15), calls=%async_computation.4 | async-start | bytes 2048 | tf_op jit(solution)/shard_map/slice | solution.py:418
  0.9 7.9 %collective-permute-start = (bf16[1,32,1024]{2,1,0:T(8,128)(2,1)S(1)}, bf16[1,32,1024]{2,1,0:T(8,128)(2,1)S(1)}, u32[]{:S(2)}, u32[]{:S(2)}) collective-permute-start(bf16[1,32,1024]{2,1,0:T(8,128)(2,1)S(1)} %dynamic-slice_bitcast_fusion), channel_id=1, source_target_pairs={{0,16},{2,18},{4,20},{6,22},{8,24},{10,26},{12,28},{14,30},{16,0},... | collective-permute-start | bytes 196616 | tf_op jit(solution)/shard_map/ppermute | solution.py:382
  8.8 30.8 %all-to-all-start = ((bf16[16,2,8,2048]{3,2,1,0:T(8,128)(2,1)}), bf16[16,2,8,2048]{3,2,1,0:T(8,128)(2,1)S(1)}, u32[]{:S(2)}, u32[]{:S(2)}) async-start(bf16[16,2,8,2048]{3,2,1,0:T(8,128)(2,1)} %shard_map.92), calls=%async_computation | async-start | bytes 2097152 | tf_op jit(solution)/shard_map/all_to_all | solution.py:410
  15.4 24.2 %collective-permute-start.1 = (bf16[2,32,1024]{2,1,0:T(8,128)(2,1)S(1)}, bf16[2,32,1024]{2,1,0:T(8,128)(2,1)S(1)}, u32[]{:S(2)}, u32[]{:S(2)}) collective-permute-start(bf16[2,32,1024]{2,1,0:T(8,128)(2,1)S(1)} %maximum_bitcast_fusion), channel_id=1, source_target_pairs={{0,8},{2,10},{4,12},{6,14},{8,0},{10,2},{12,4},{14,6},{16,24},{18,... | collective-permute-start | bytes 393224 | tf_op jit(solution)/shard_map/ppermute | solution.py:382
  17.9 27.5 %copy-start.6 = (s32[4]{0:T(128)S(1)}, s32[4]{0:T(128)}, u32[]{:S(2)}) copy-start(s32[4]{0:T(128)} %refs_1_.9) | copy-start | bytes 52
  39.6 28.8 %all-to-all-start.1 = ((bf16[16,2,8,2048]{3,2,1,0:T(8,128)(2,1)}), bf16[16,2,8,2048]{3,2,1,0:T(8,128)(2,1)S(1)}, u32[]{:S(2)}, u32[]{:S(2)}) async-start(bf16[16,2,8,2048]{3,2,1,0:T(8,128)(2,1)} %get-tuple-element.39), calls=%async_computation.1 | async-start | bytes 2097152 | tf_op jit(solution)/shard_map/all_to_all | solution.py:410
  61.1 3.7 %collective-permute-start.2 = (bf16[16,2,8,2048]{3,2,1,0:T(8,128)(2,1)S(1)}, bf16[16,2,8,2048]{3,2,1,0:T(8,128)(2,1)S(1)}, u32[]{:S(2)}, u32[]{:S(2)}) collective-permute-start(bf16[16,2,8,2048]{3,2,1,0:T(8,128)(2,1)S(1)} %get-tuple-element.45), channel_id=1, source_target_pairs={{0,1},{1,0},{2,3},{3,2},{4,5},{5,4},{6,7},{7,6},{8,9},{9,8},{10,11... | collective-permute-start | bytes 3145736 | tf_op jit(solution)/shard_map/ppermute | solution.py:446
  61.3 29.2 %copy-start.11 = (bf16[2,2,32,1024]{3,2,1,0:T(8,128)(2,1)}, bf16[2,2,32,1024]{3,2,1,0:T(8,128)(2,1)S(1)}, u32[]{:S(2)}) copy-start(bf16[2,2,32,1024]{3,2,1,0:T(8,128)(2,1)S(1)} %pad_maximum_fusion.1) | copy-start | bytes 786436
  61.3 29.2 %collective-permute-start.5 = (bf16[4,32,1024]{2,1,0:T(8,128)(2,1)S(1)}, bf16[4,32,1024]{2,1,0:T(8,128)(2,1)S(1)}, u32[]{:S(2)}, u32[]{:S(2)}) collective-permute-start(bf16[4,32,1024]{2,1,0:T(8,128)(2,1)S(1)} %bitcast.32), channel_id=1, source_target_pairs={{0,6},{2,4},{4,2},{6,0},{8,14},{10,12},{12,10},{14,8},{16,22},{18,... | collective-permute-start | bytes 786440 | tf_op jit(solution)/shard_map/ppermute | solution.py:382
  64.2 26.3 %collective-permute-start.4 = (bf16[4,32,1024]{2,1,0:T(8,128)(2,1)S(1)}, bf16[4,32,1024]{2,1,0:T(8,128)(2,1)S(1)}, u32[]{:S(2)}, u32[]{:S(2)}) collective-permute-start(bf16[4,32,1024]{2,1,0:T(8,128)(2,1)S(1)} %bitcast.33), channel_id=1, source_target_pairs={{0,4},{2,6},{4,0},{6,2},{8,12},{10,14},{12,8},{14,10},{16,20},{18,... | collective-permute-start | bytes 786440 | tf_op jit(solution)/shard_map/ppermute | solution.py:382
  64.7 25.8 %collective-permute-start.3 = (bf16[4,32,1024]{2,1,0:T(8,128)(2,1)S(1)}, bf16[4,32,1024]{2,1,0:T(8,128)(2,1)}, u32[]{:S(2)}, u32[]{:S(2)}) collective-permute-start(bf16[4,32,1024]{2,1,0:T(8,128)(2,1)S(1)} %bitcast.34), channel_id=1, source_target_pairs={{0,2},{2,0},{4,6},{6,4},{8,10},{10,8},{12,14},{14,12},{16,18},{18,... | collective-permute-start | bytes 786440 | tf_op jit(solution)/shard_map/ppermute | solution.py:382
  68.4 29.3 %all-to-all-start.2 = ((bf16[16,2,8,2048]{3,2,1,0:T(8,128)(2,1)}), bf16[16,2,8,2048]{3,2,1,0:T(8,128)(2,1)S(1)}, u32[]{:S(2)}, u32[]{:S(2)}) async-start(bf16[16,2,8,2048]{3,2,1,0:T(8,128)(2,1)} %add_convert_fusion.1), calls=%async_computation.2 | async-start | bytes 2097152 | tf_op jit(solution)/shard_map/all_to_all | solution.py:410
  90.5 7.3 %copy-start.12 = (bf16[4,32,1024]{2,1,0:T(8,128)(2,1)}, bf16[4,32,1024]{2,1,0:T(8,128)(2,1)S(1)}, u32[]{:S(2)}) copy-start(bf16[4,32,1024]{2,1,0:T(8,128)(2,1)S(1)} %collective-permute-done.5) | copy-start | bytes 786436
  90.5 7.3 %copy-start.13 = (bf16[4,32,1024]{2,1,0:T(8,128)(2,1)}, bf16[4,32,1024]{2,1,0:T(8,128)(2,1)S(1)}, u32[]{:S(2)}) copy-start(bf16[4,32,1024]{2,1,0:T(8,128)(2,1)S(1)} %collective-permute-done.4) | copy-start | bytes 786436
  90.5 2.7 %collective-permute-start.6 = (bf16[16,2,8,2048]{3,2,1,0:T(8,128)(2,1)S(1)}, bf16[16,2,8,2048]{3,2,1,0:T(8,128)(2,1)S(1)}, u32[]{:S(2)}, u32[]{:S(2)}) collective-permute-start(bf16[16,2,8,2048]{3,2,1,0:T(8,128)(2,1)S(1)} %get-tuple-element.53), channel_id=1, source_target_pairs={{0,1},{1,0},{2,3},{3,2},{4,5},{5,4},{6,7},{7,6},{8,9},{9,8},{10,11... | collective-permute-start | bytes 3145736 | tf_op jit(solution)/shard_map/ppermute | solution.py:446
  94.6 11.6 %copy-start.5 = (f32[8]{0:T(128)S(1)}, f32[8]{0:T(128)}, u32[]{:S(2)}) copy-start(f32[8]{0:T(128)} %refs_1_.11) | copy-start | bytes 100
  94.6 14.3 %copy-start.7 = (s32[64]{0:T(128)S(1)}, s32[64]{0:T(128)}, u32[]{:S(2)}) copy-start(s32[64]{0:T(128)} %refs_0_.5) | copy-start | bytes 772
  97.8 7.4 %copy-start.1 = (bf16[16,2,8,2048]{3,2,1,0:T(8,128)(2,1)}, bf16[16,2,8,2048]{3,2,1,0:T(8,128)(2,1)S(1)}, u32[]{:S(2)}) copy-start(bf16[16,2,8,2048]{3,2,1,0:T(8,128)(2,1)S(1)} %all-to-all-done.2) | copy-start | bytes 3145732
  97.8 28.9 %all-to-all-start.3 = ((bf16[16,2,8,2048]{3,2,1,0:T(8,128)(2,1)}), bf16[16,2,8,2048]{3,2,1,0:T(8,128)(2,1)S(1)}, u32[]{:S(2)}, u32[]{:S(2)}) async-start(bf16[16,2,8,2048]{3,2,1,0:T(8,128)(2,1)} %add_convert_fusion), calls=%async_computation.3 | async-start | bytes 2097152 | tf_op jit(solution)/shard_map/all_to_all | solution.py:410
  105.2 2.7 %collective-permute-start.7 = (bf16[1,16,32,1024]{3,2,1,0:T(8,128)(2,1)S(1)}, bf16[1,16,32,1024]{3,2,1,0:T(8,128)(2,1)S(1)}, u32[]{:S(2)}, u32[]{:S(2)}) collective-permute-start(bf16[1,16,32,1024]{3,2,1,0:T(8,128)(2,1)S(1)} %bitcast.29), channel_id=1, source_target_pairs={{0,1},{1,0},{2,3},{3,2},{4,5},{5,4},{6,7},{7,6},{8,9},{9,8},{10,11... | collective-permute-start | bytes 3145736 | tf_op jit(solution)/shard_map/ppermute | solution.py:382
  105.3 1.0 copy-start.3
  107.9 1.0 copy-start.9
  108.9 1.2 copy-start.2
  110.1 1.2 copy-start.4
  111.3 1.6 %copy-start.8 = (bf16[64,8,2048]{2,1,0:T(8,128)(2,1)S(1)}, bf16[64,8,2048]{2,1,0:T(8,128)(2,1)}, u32[]{:S(2)}) copy-start(bf16[64,8,2048]{2,1,0:T(8,128)(2,1)} %get-tuple-element.36.refs_2_) | copy-start | bytes 6291460
  112.9 1.2 copy-start.10
